TPU v7x, 768 devices: a whole 4x8x12 slice. The times are simulated.
768 devices in a mesh: users: 96 (over x, z, core), items: 8 (over y).
Axes of the slice: x: 4, y: 8, z: 12, core: 2. Of those that a mesh axis runs over, the one named last changes fastest.
Arguments:
- user_factors: float32 [49152, 512], P('users'), may hold values from -6 to 6
- item_factors: bfloat16 [8, 12288, 512], P('items', 'users'), may hold values from -0.25 to 0.25
- tile_weights: bfloat16 [96, 8, 16, 128, 128], P('users', 'items'), may hold values from 0 to 4, as said below
- tile_scores: bfloat16 [96, 8, 16, 128, 128], P('users', 'items'), may hold values from -6 to 6
- tile_users: int32 [96, 8, 16], P('users', 'items'), may hold values from 0 to 3
- tile_items: int32 [96, 8, 16], P('users', 'items'), may hold values from 0 to 95
- tile_count: int32 [96, 8], P('users', 'items'), may hold values from 4 to 16, as said below
Outputs:
- new_factors: float32 [49152, 512], P('users')
Inputs may be any that keep to these rules, and one draw needn't show every extreme that they name: `tile_count`: every device's list has between a quarter of 16 and 16 live slots, and one device has all 16 live in every draw. `tile_weights`: about half of the entries are zero.
All inputs are finite; a program needn't handle non-finite values.
Results may differ from a plain program's by a relative error of at most 0.00088.
The roundings to bfloat16 on the way count: a program that leaves them out, or rounds other values in their place, can miss the bound.
Values may be sent and summed in bfloat16 or wider, within the bound.
No kernel may reach another device: no remote copies, remote signals or barrier semaphores. Data moves between devices by JAX's collectives and lax.ppermute only.
A program may use at most 64 MiB of HBM per device.

v0:
```python
import jax
import jax.numpy as jnp
from jax import lax
from jax.sharding import PartitionSpec as P

D = 512
BLK = 128
SWEEP = 2
CG_STEPS = 3
UB_DEV = 4


implicit_scale = 8.0
ridge_weight = 1.0


def tile_terms(rows_bf, live_weights, hblocks):
    scores = jnp.einsum("tuk,tik->tui", rows_bf, hblocks, preferred_element_type=jnp.float32)
    scaled = (scores * live_weights).astype(jnp.bfloat16)
    return jnp.einsum("tui,tik->tuk", scaled, hblocks, preferred_element_type=jnp.float32)


def owner_rows(owners, terms):
    partial_rows = jnp.einsum("tb,tuk->buk", owners, terms, precision=lax.Precision.HIGHEST)
    return partial_rows.reshape(-1, BLK)


def group_total(owners, terms):
    return lax.psum(owner_rows(owners, terms), "items")


def local(
    user_factors, item_factors, tile_weights, tile_scores, tile_users, tile_items, tile_count
):
    n_users = lax.axis_size("users")
    n_items = lax.axis_size("items")
    width = SWEEP * BLK
    total_items = item_factors.shape[1] * n_users * n_items
    implicit = implicit_scale * D / total_items
    own_items = item_factors[0]
    own_slice = own_items[:, :width]
    partial_gram = lax.dot_general(
        own_slice, own_items, (((0,), (0,)), ((), ())), preferred_element_type=jnp.float32
    )
    gram = lax.psum(partial_gram, ("users", "items"))
    user_idx = tile_users[0, 0]
    item_idx = tile_items[0, 0]
    live = jnp.arange(tile_weights.shape[2]) < tile_count[0, 0]
    live_weights = tile_weights[0, 0] * live[:, None, None].astype(jnp.bfloat16)
    owners = (user_idx[:, None] == jnp.arange(UB_DEV)[None, :]).astype(jnp.float32)
    predicted = tile_scores[0, 0].astype(jnp.float32)
    group_slice = lax.all_gather(own_slice, "users", axis=0, tiled=True)
    factors = user_factors
    for block in range(SWEEP):
        low = block * BLK
        high = low + BLK
        columns = group_slice[:, low:high]
        hblocks = columns.reshape(-1, BLK, BLK)[item_idx]
        gram_rows = gram[low:high]
        gram_diag = gram_rows[:, low:high]
        current = factors[:, low:high]
        errors = ((predicted - 1.0) * live_weights).astype(jnp.bfloat16)
        error_terms = jnp.einsum(
            "tui,tik->tuk", errors, hblocks, preferred_element_type=jnp.float32
        )
        local_grad = (
            implicit * jnp.dot(factors, gram_rows.T, precision=lax.Precision.HIGHEST)
            + ridge_weight * current
        )
        grad = local_grad + group_total(owners, error_terms)
        resid = -grad
        direction = resid
        delta = jnp.zeros_like(resid)
        norm_now = jnp.sum(resid * resid, axis=1, keepdims=True)
        for step in range(CG_STEPS):
            dir_whole = direction.astype(jnp.bfloat16)
            dir_bf = dir_whole.reshape(UB_DEV, BLK, BLK)[user_idx]
            local_part = (
                implicit * jnp.dot(direction, gram_diag, precision=lax.Precision.HIGHEST)
                + ridge_weight * direction
            )
            image = local_part + group_total(owners, tile_terms(dir_bf, live_weights, hblocks))
            alpha = norm_now / jnp.sum(direction * image, axis=1, keepdims=True)
            delta = delta + alpha * direction
            resid = resid - alpha * image
            if step + 1 < CG_STEPS:
                norm_next = jnp.sum(resid * resid, axis=1, keepdims=True)
                direction = resid + norm_next / norm_now * direction
                norm_now = norm_next
        factors = factors.at[:, low:high].set(current + delta)
        if block + 1 < SWEEP:
            delta_whole = delta.astype(jnp.bfloat16)
            step_rows = delta_whole.reshape(UB_DEV, BLK, BLK)[user_idx]
            predicted = predicted + jnp.einsum(
                "tuk,tik->tui", step_rows, hblocks, preferred_element_type=jnp.float32
            )
    return factors


def solution(mesh):
    placed = (
        P("users", None),
        P("items", "users", None),
        P("users", "items", None, None, None),
        P("users", "items", None, None, None),
        P("users", "items", None),
        P("users", "items", None),
        P("users", "items"),
    )
    return jax.shard_map(
        local, mesh=mesh, in_specs=placed, out_specs=P("users", None), check_vma=False
    )
```

profile of v0, /device:TPU:1, one launch (start us, length us, event | category | flops | bytes accessed | tf_op | source)
XLA Modules:
  0.0 1217.2 jit_solution(12031608743705781826)
XLA Ops:
  7.4 1.5 slice.91
  8.9 2.1 fusion.58
  12.4 1.6 copy.34
  14.0 126.4 %all-gather.2.cloned.1.call-done = bf16[12288,256]{1,0:T(8,128)(2,1)} async-done(((bf16[128,256]{1,0:T(8,128)(2,1)}), bf16[12288,256]{1,0:T(8,128)(2,1)}) %all-gather.2.cloned.1.call-update) | async-done | bytes 6291472 | tf_op jit(solution)/shard_map/all_gather | solution.py:52
  140.4 4.8 fusion.84
  145.2 2.5 gather_fusion
  147.8 1.3 fusion.37
  149.1 1.7 copy.48
  151.3 0.7 copy.114
  152.1 329.9 %all-reduce.10.cloned.1.call-done = f32[256,512]{1,0:T(8,128)} async-done(((f32[256,512]{1,0:T(8,128)}), f32[256,512]{1,0:T(8,128)}) %all-reduce.10.cloned.1.call-update) | async-done | bytes 524304 | tf_op jit(solution)/shard_map/psum | solution.py:45
  482.0 78.1 %all-reduce.12.cloned.1.call-done = f32[512,128]{0,1:T(8,128)} async-done(((f32[512,128]{0,1:T(8,128)}), f32[512,128]{0,1:T(8,128)}) %all-reduce.12.cloned.1.call-update) | async-done | bytes 262160 | tf_op jit(solution)/shard_map/psum | solution.py:29
  560.1 2.5 negate_convert_fusion.1
  563.4 1.6 fusion.13
  565.0 2.6 copy.52
  567.6 1.7 fusion.75
  569.3 0.7 copy.113
  570.1 82.0 %all-reduce.14.cloned.1.call-done = f32[512,128]{0,1:T(8,128)} async-done(((f32[512,128]{0,1:T(8,128)}), f32[512,128]{0,1:T(8,128)}) %all-reduce.14.cloned.1.call-update) | async-done | bytes 262160 | tf_op jit(solution)/shard_map/psum | solution.py:29
  652.2 1.5 multiply_reduce_fusion.8
  653.9 1.4 gather_fusion.2
  655.3 2.6 fusion.12
  658.0 2.6 copy.56
  660.6 1.7 fusion.73
  662.3 0.7 copy.112
  663.1 82.1 %all-reduce.16.cloned.1.call-done = f32[512,128]{0,1:T(8,128)} async-done(((f32[512,128]{0,1:T(8,128)}), f32[512,128]{0,1:T(8,128)}) %all-reduce.16.cloned.1.call-update) | async-done | bytes 262160 | tf_op jit(solution)/shard_map/psum | solution.py:29
  745.2 1.4 multiply_reduce_fusion.6
  747.5 1.5 gather_fusion.3
  749.0 2.6 fusion.11
  751.6 2.6 copy.59
  754.3 1.7 fusion.71
  756.0 0.7 copy.111
  756.7 2.7 gather_fusion.5
  759.4 79.4 %all-reduce.18.cloned.1.call-done = f32[512,128]{0,1:T(8,128)} async-done(((f32[512,128]{0,1:T(8,128)}), f32[512,128]{0,1:T(8,128)}) %all-reduce.18.cloned.1.call-update) | async-done | bytes 262160 | tf_op jit(solution)/shard_map/psum | solution.py:29
  838.8 1.4 fusion.34
  840.2 0.8 fusion.81
  841.2 0.8 gather_fusion.4
  842.0 2.7 fusion.14
  844.7 2.7 copy.63
  847.4 1.7 fusion.69
  849.1 0.7 copy.110
  850.7 0.7 fusion.43
  851.5 80.4 %all-reduce.20.cloned.1.call-done = f32[512,128]{0,1:T(8,128)} async-done(((f32[512,128]{0,1:T(8,128)}), f32[512,128]{0,1:T(8,128)}) %all-reduce.20.cloned.1.call-update) | async-done | bytes 262160 | tf_op jit(solution)/shard_map/psum | solution.py:29
  931.9 1.7 negate_convert_fusion
  933.7 0.8 gather_fusion.6
  934.5 1.6 fusion.10
  936.1 2.6 copy.67
  938.7 1.7 fusion.67
  940.4 0.7 copy.109
  941.2 82.0 %all-reduce.22.cloned.1.call-done = f32[512,128]{0,1:T(8,128)} async-done(((f32[512,128]{0,1:T(8,128)}), f32[512,128]{0,1:T(8,128)}) %all-reduce.22.cloned.1.call-update) | async-done | bytes 262160 | tf_op jit(solution)/shard_map/psum | solution.py:29
  1023.3 1.5 multiply_reduce_fusion.3
  1025.0 0.8 gather_fusion.7
  1025.8 1.6 fusion.9
  1027.4 2.6 copy.71
  1030.0 1.7 fusion.65
  1031.7 0.7 copy.108
  1032.5 82.1 %all-reduce.24.cloned.1.call-done = f32[512,128]{0,1:T(8,128)} async-done(((f32[512,128]{0,1:T(8,128)}), f32[512,128]{0,1:T(8,128)}) %all-reduce.24.cloned.1.call-update) | async-done | bytes 262160 | tf_op jit(solution)/shard_map/psum | solution.py:29
  1114.6 1.4 multiply_reduce_fusion.1
  1116.9 1.5 gather_fusion.8
  1118.4 2.6 fusion.8
  1121.1 1.7 copy.74
  1123.3 0.7 copy.107
  1124.7 81.5 %all-reduce.26.cloned.1.call-done = f32[512,128]{0,1:T(8,128)} async-done(((f32[512,128]{0,1:T(8,128)}), f32[512,128]{0,1:T(8,128)}) %all-reduce.26.cloned.1.call-update) | async-done | bytes 262160 | tf_op jit(solution)/shard_map/psum | solution.py:29
  1206.1 1.4 fusion.35
  1207.6 0.7 fusion.44
  1208.3 1.3 copy.46
  (81 shorter events, 6.9 us)
Async XLA Ops:
  7.4 133.0 %all-gather.2.cloned.1.call-start = ((), (), s32[]{:S(2)}) async-start(), calls=%async_computation.1 | async-start | bytes 6356992 | tf_op jit(solution)/shard_map/all_gather | solution.py:52
  8.9 473.1 %all-reduce.10.cloned.1.call-start = ((), (), s32[]{:S(2)}) async-start(), calls=%async_computation | async-start | bytes 1048576 | tf_op jit(solution)/shard_map/psum | solution.py:45
  11.0 549.1 %all-reduce.12.cloned.1.call-start = ((), (), s32[]{:S(2)}) async-start(), calls=%async_computation.2 | async-start | bytes 524288 | tf_op jit(solution)/shard_map/psum | solution.py:29
  11.8 133.4 %copy-start.12 = (s32[1024]{0:T(1024)}, s32[1024]{0:T(1024)S(1)}, u32[]{:S(2)}) copy-start(s32[1024]{0:T(1024)S(1)} %pad_clamp_fusion.1) | copy-start | bytes 12292
  14.0 133.7 %copy-start = (bf16[1,1,16,128,128]{4,3,2,1,0:T(8,128)(2,1)S(1)}, bf16[1,1,16,128,128]{4,3,2,1,0:T(8,128)(2,1)}, u32[]{:S(2)}) copy-start(bf16[1,1,16,128,128]{4,3,2,1,0:T(8,128)(2,1)} %param.13) | copy-start | bytes 1572868
  14.0 133.7 %copy-start.1 = (bf16[1,1,16,128,128]{4,3,2,1,0:T(8,128)(2,1)S(1)}, bf16[1,1,16,128,128]{4,3,2,1,0:T(8,128)(2,1)}, u32[]{:S(2)}) copy-start(bf16[1,1,16,128,128]{4,3,2,1,0:T(8,128)(2,1)} %param.14) | copy-start | bytes 1572868
  145.2 5.7 copy-start.4
  152.0 500.1 %all-reduce.14.cloned.1.call-start = ((), (), s32[]{:S(2)}) async-start(), calls=%async_computation.3 | async-start | bytes 524288 | tf_op jit(solution)/shard_map/psum | solution.py:29
  152.1 501.8 %copy-start.11 = (s32[1024]{0:T(1024)}, s32[1024]{0:T(1024)S(1)}, u32[]{:S(2)}) copy-start(s32[1024]{0:T(1024)S(1)} %pad_clamp_fusion) | copy-start | bytes 12292
  570.1 175.1 %all-reduce.16.cloned.1.call-start = ((), (), s32[]{:S(2)}) async-start(), calls=%async_computation.4 | async-start | bytes 524288 | tf_op jit(solution)/shard_map/psum | solution.py:29
  663.0 175.7 %all-reduce.18.cloned.1.call-start = ((), (), s32[]{:S(2)}) async-start(), calls=%async_computation.5 | async-start | bytes 524288 | tf_op jit(solution)/shard_map/psum | solution.py:29
  746.7 0.6 copy-start.7
  751.6 88.6 %copy-start.8 = (f32[512]{0:T(512)S(1)}, f32[512]{0:T(512)}, u32[]{:S(2)}) copy-start(f32[512]{0:T(512)} %copy-done.7) | copy-start | bytes 6148
  756.7 175.2 %all-reduce.20.cloned.1.call-start = ((), (), s32[]{:S(2)}) async-start(), calls=%async_computation.6 | async-start | bytes 524288 | tf_op jit(solution)/shard_map/psum | solution.py:29
  842.0 8.8 copy-start.3
  844.7 87.2 %copy-start.2 = (f32[256,512]{1,0:T(8,128)S(1)}, f32[256,512]{1,0:T(8,128)}, u32[]{:S(2)}) copy-start(f32[256,512]{1,0:T(8,128)} %all-reduce.10.cloned.1.call-done) | copy-start | bytes 1572868
  849.8 173.5 %all-reduce.22.cloned.1.call-start = ((), (), s32[]{:S(2)}) async-start(), calls=%async_computation.7 | async-start | bytes 524288 | tf_op jit(solution)/shard_map/psum | solution.py:29
  941.2 173.4 %all-reduce.24.cloned.1.call-start = ((), (), s32[]{:S(2)}) async-start(), calls=%async_computation.8 | async-start | bytes 524288 | tf_op jit(solution)/shard_map/psum | solution.py:29
  1024.7 5.3 copy-start.5
  1032.5 173.7 %all-reduce.26.cloned.1.call-start = ((), (), s32[]{:S(2)}) async-start(), calls=%async_computation.9 | async-start | bytes 524288 | tf_op jit(solution)/shard_map/psum | solution.py:29
  1116.1 0.6 copy-start.9
  1121.1 86.5 %copy-start.10 = (f32[512]{0:T(512)S(1)}, f32[512]{0:T(512)}, u32[]{:S(2)}) copy-start(f32[512]{0:T(512)} %copy-done.9) | copy-start | bytes 6148
  1121.1 86.5 %copy-start.6 = (f32[512]{0:T(512)S(1)}, f32[512]{0:T(512)}, u32[]{:S(2)}) copy-start(f32[512]{0:T(512)} %copy-done.5) | copy-start | bytes 6148
Sparse Core Ops, SparseCore 0:
  12.5 127.9 all-gather.1
Sparse Core Ops, SparseCore 1:
  14.7 467.2 all-reduce.9
  484.3 75.7 all-reduce.11
  570.2 82.0 all-reduce.13
  663.1 82.0 all-reduce.15
  756.8 82.0 all-reduce.17
  849.9 82.0 all-reduce.19
  941.2 82.0 all-reduce.21
  1032.5 82.0 all-reduce.23
  1124.1 82.0 all-reduce.25
where the time goes:
time: 1220 us
  waiting for transfers between devices  1100 us (90%)
  local copies, waits for them, and re-layouts  48.8 us (4%)
  matrix products  42.8 us (4%)
  between operations  16.2 us (1%)
    psum x8, waiting for transfers between devices, group_total(): return lax.psum(owner_rows(owners, terms), 'items')  648 us
    psum x1, waiting for transfers between devices, local(): gram = lax.psum(partial_gram, ('users', 'items'))  330 us
    all_gather x1, waiting for transfers between devices, local(): group_slice = lax.all_gather(own_slice, 'users', axis=0, tiled=True)  126 us
  transfers between devices with their start and end apart: 10, of which 10 were waited for; matrix products, arithmetic and copies ran while one was open for 2% of the time, Pallas kernels for 0%

commit v1 on v0

v1 whole, which is shorter than its diff:
```python
import functools

import jax
import jax.numpy as jnp
from jax import lax
from jax.experimental import pallas as pl
from jax.experimental.pallas import tpu as pltpu
from jax.sharding import Mesh
from jax.sharding import PartitionSpec as P

D = 512
BLK = 128
SWEEP = 2
CG_STEPS = 3
UB_DEV = 4

implicit_scale = 8.0
ridge_weight = 1.0

X_CHIPS = 4
CORES = 2

NT = (((1,), (1,)), ((), ()))
NN = (((1,), (0,)), ((), ()))
TN = (((0,), (0,)), ((), ()))


def spread(value, axis):
    n = lax.axis_size(axis)
    copies = jnp.broadcast_to(value[None], (n,) + value.shape)
    return lax.all_to_all(copies, axis, 0, 0)


def swap_cores(value):
    return lax.ppermute(value, "core", [(0, 1), (1, 0)])


def pick_kernel(place_ref, mine_ref, other_ref, out_ref, sems):
    tiles = place_ref.shape[0]
    per_core = mine_ref.shape[0]

    def copy(source, row, t):
        return pltpu.make_async_copy(
            source.at[row],
            out_ref.at[pl.ds((t // 2) * BLK, BLK), pl.ds((t % 2) * BLK, BLK)],
            sems.at[t],
        )

    for t in range(tiles):
        place = place_ref[t]

        @pl.when(place < per_core)
        def _():
            copy(mine_ref, place, t).start()

        @pl.when(place >= per_core)
        def _():
            copy(other_ref, place - per_core, t).start()

    for t in range(tiles):
        copy(mine_ref, 0, t).wait()


def pick(place, mine, other):
    tiles = place.shape[0]
    return pl.pallas_call(
        pick_kernel,
        out_shape=jax.ShapeDtypeStruct((tiles // 2 * BLK, 2 * BLK), jnp.bfloat16),
        in_specs=[
            pl.BlockSpec(memory_space=pltpu.SMEM),
            pl.BlockSpec(memory_space=pl.ANY),
            pl.BlockSpec(memory_space=pl.ANY),
        ],
        out_specs=pl.BlockSpec(memory_space=pltpu.VMEM),
        scratch_shapes=[pltpu.SemaphoreType.DMA((tiles,))],
        name="pick",
    )(place, mine, other)


def widen_kernel(owner_ref, pack_ref, wide_ref):
    groups = pack_ref.shape[0]
    tiles = owner_ref.shape[0] // groups

    for pair in range(tiles // 2):

        def body(group, carry):
            rows = []
            for half in range(2):
                t = 2 * pair + half
                owner = owner_ref[group * tiles + t]
                weights = pack_ref[group, t].astype(jnp.float32)
                for block in range(UB_DEV):
                    keep = (owner == block).astype(jnp.float32)
                    rows.append(weights * keep)
            column = pl.multiple_of((group * (tiles // 2) + pair) * BLK, BLK)
            wide_ref[:, pl.ds(column, BLK)] = jnp.concatenate(rows, axis=0).astype(jnp.bfloat16)
            return carry

        lax.fori_loop(0, groups, body, 0)


def widen(owner, pack):
    groups, _, own, _ = pack.shape
    rows = 2 * UB_DEV * own
    return pl.pallas_call(
        widen_kernel,
        out_shape=jax.ShapeDtypeStruct((rows, owner.shape[0] // 2 * BLK), jnp.bfloat16),
        in_specs=[
            pl.BlockSpec(memory_space=pltpu.SMEM),
            pl.BlockSpec(memory_space=pltpu.VMEM),
        ],
        out_specs=pl.BlockSpec(memory_space=pltpu.VMEM),
        name="widen",
    )(owner, pack)


def exact_dot(left, right, dims):
    return lax.dot_general(
        left, right, dims, precision=lax.Precision.HIGHEST, preferred_element_type=jnp.float32
    )


def solve_kernel(
    low, implicit, last, factors_ref, gram_ref, table_ref, wide_ref, side_ref, *rest
):
    if last:
        (out_ref,) = rest
    else:
        out_ref, errors_ref = rest
    users = factors_ref.shape[0]
    rows, columns = wide_ref.shape
    width = 1024
    chunks = columns // width
    tiles = width // BLK

    def pieces(c):
        at = pl.ds(c * width, width)
        return table_ref[at, :], wide_ref[:, at].astype(jnp.float32)

    def scores(c):
        parts = []
        for pair in range(tiles):
            halves = [side_ref[c, 2 * tiles + 2 * pair + half] for half in range(2)]
            parts.append(jnp.concatenate([h for h in halves for _ in range(UB_DEV)], axis=0))
        return jnp.concatenate(parts, axis=1).astype(jnp.float32)

    def fold(total):
        return total[:users, :BLK] + total[users:, BLK:]

    def pair_rows(value):
        value = value.astype(jnp.bfloat16)
        none = jnp.zeros_like(value)
        return jnp.concatenate(
            [jnp.concatenate([value, none], axis=1), jnp.concatenate([none, value], axis=1)], axis=0
        )

    def tile_terms(direction):
        both = pair_rows(direction)
        total = jnp.zeros((rows, 2 * BLK), jnp.float32)
        for c in range(chunks):
            table, weights = pieces(c)
            seen = lax.dot_general(both, table, NT, preferred_element_type=jnp.float32)
            scaled = (seen * weights).astype(jnp.bfloat16)
            total += lax.dot_general(scaled, table, NN, preferred_element_type=jnp.float32)
        return fold(total)

    total = jnp.zeros((rows, 2 * BLK), jnp.float32)
    for c in range(chunks):
        table, weights = pieces(c)
        if low == 0:
            errors = ((scores(c) - 1.0) * weights).astype(jnp.bfloat16)
        else:
            errors = side_ref[:, pl.ds(c * width, width)]
        total += lax.dot_general(errors, table, NN, preferred_element_type=jnp.float32)

    factors = factors_ref[...]
    current = factors[:, low : low + BLK]
    gram_rows = gram_ref[low : low + BLK, :]
    gram_diag = gram_rows[:, low : low + BLK]
    grad = implicit * exact_dot(factors, gram_rows, NT) + ridge_weight * current + fold(total)
    resid = -grad
    direction = resid
    delta = jnp.zeros_like(resid)
    norm_now = jnp.sum(resid * resid, axis=1, keepdims=True)
    for step in range(CG_STEPS):
        local_part = implicit * exact_dot(direction, gram_diag, NN) + ridge_weight * direction
        image = local_part + tile_terms(direction)
        alpha = norm_now / jnp.sum(direction * image, axis=1, keepdims=True)
        delta = delta + alpha * direction
        resid = resid - alpha * image
        if step + 1 < CG_STEPS:
            norm_next = jnp.sum(resid * resid, axis=1, keepdims=True)
            direction = resid + norm_next / norm_now * direction
            norm_now = norm_next
    if low:
        out_ref[:, :low] = factors[:, :low]
    out_ref[:, low : low + BLK] = current + delta
    if last:
        return
    out_ref[:, low + BLK :] = factors[:, low + BLK :]
    both = pair_rows(delta)
    for c in range(chunks):
        table, weights = pieces(c)
        seen = lax.dot_general(both, table, NT, preferred_element_type=jnp.float32)
        predicted = scores(c) + seen
        errors_ref[:, pl.ds(c * width, width)] = ((predicted - 1.0) * weights).astype(jnp.bfloat16)


def solve(block, implicit, factors, gram, table, wide, side):
    last = block + 1 == SWEEP
    users = factors.shape[0]
    out_width = SWEEP * BLK if last else D
    shapes = [jax.ShapeDtypeStruct((users, out_width), jnp.float32)]
    if not last:
        shapes.append(jax.ShapeDtypeStruct(wide.shape, jnp.bfloat16))
    return pl.pallas_call(
        functools.partial(solve_kernel, block * BLK, implicit, last),
        out_shape=shapes,
        in_specs=[pl.BlockSpec(memory_space=pltpu.VMEM)] * 5,
        out_specs=[pl.BlockSpec(memory_space=pltpu.VMEM)] * len(shapes),
        compiler_params=pltpu.CompilerParams(vmem_limit_bytes=40 * 1024 * 1024),
        name="solve%d" % block,
    )(factors, gram, table, wide, side)


def local(
    user_factors, item_factors, tile_weights, tile_scores, tile_users, tile_items, tile_count
):
    n_items = lax.axis_size("items")
    n_x = lax.axis_size("x")
    n_z = lax.axis_size("z")
    tiles = tile_weights.shape[2]
    own = BLK // n_items
    width = SWEEP * BLK
    total_items = item_factors.shape[1] * n_x * n_z * CORES * n_items
    implicit = implicit_scale * D / total_items
    core = lax.axis_index("core")
    group = lax.axis_index("items")
    own_items = item_factors[0]

    line = lax.all_gather(own_items, "z", axis=0)
    item_idx = tile_items[0, 0]
    chip_block = item_idx // CORES
    place = chip_block + (item_idx % CORES != core).astype(jnp.int32) * (n_x * n_z)

    def group_blocks(line_columns):
        mine = spread(line_columns, "x").reshape(n_x * n_z, BLK, BLK)
        other = swap_cores(mine)
        return lax.all_gather(pick(place, mine, other), "items", axis=0, tiled=True)

    table0 = group_blocks(spread(own_items[:, :BLK], "z"))
    table1 = group_blocks(line[:, :, BLK:width])

    live = jnp.arange(tiles) < tile_count[0, 0]
    live_weights = tile_weights[0, 0] * live[:, None, None].astype(jnp.bfloat16)
    owner_rows = jnp.broadcast_to(
        tile_users[0, 0].astype(jnp.bfloat16)[None, None, :, None], (n_items, 1, tiles, BLK)
    )
    owner_rows = jnp.pad(owner_rows, ((0, 0), (0, 0), (0, own - tiles), (0, 0)))

    def by_user(value):
        return value.reshape(tiles, n_items, own, BLK).transpose(1, 0, 2, 3)

    pack = jnp.concatenate([by_user(live_weights), by_user(tile_scores[0, 0]), owner_rows], axis=1)
    pack = lax.all_to_all(pack, "items", 0, 0)
    owner = pack[:, 2 * tiles, :tiles, 0].astype(jnp.int32).reshape(-1)
    wide = widen(owner, pack)

    line_items = line.reshape(n_z * BLK, D)
    partial = lax.dot_general(
        line_items[:, :width], line_items, TN, preferred_element_type=jnp.float32
    ).reshape(CORES, BLK, D)
    half = jnp.where(core == 0, partial[0], partial[1])
    send = jnp.where(core == 0, partial[1], partial[0])
    half = half + swap_cores(send)
    shares = half.reshape(n_x * n_items, -1, D)
    share = jnp.sum(lax.all_to_all(shares, ("x", "items"), 0, 0), axis=0)
    half = spread(share, ("x", "items")).reshape(BLK, D)
    there = swap_cores(half)
    gram = jnp.concatenate(
        [jnp.where(core == 0, half, there), jnp.where(core == 0, there, half)], axis=0
    )

    factors = lax.dynamic_index_in_dim(
        user_factors.reshape(UB_DEV, n_items, own, D), group, axis=1, keepdims=False
    ).reshape(UB_DEV * own, D)
    factors, errors = solve(0, implicit, factors, gram, table0, wide, pack)
    (swept,) = solve(1, implicit, factors, gram, table1, wide, errors)
    swept = spread(swept, "items").reshape(n_items, UB_DEV, own, width)
    swept = swept.transpose(1, 0, 2, 3).reshape(-1, width)
    return jnp.concatenate([swept, user_factors[:, width:]], axis=1)


def solution(mesh):
    n_users, n_items = mesh.devices.shape
    n_z = n_users // (X_CHIPS * CORES)
    chips = Mesh(
        mesh.devices.reshape(X_CHIPS, n_z, CORES, n_items), ("x", "z", "core", "items")
    )
    users = ("x", "z", "core")
    placed = (
        P(users, None),
        P("items", users, None),
        P(users, "items", None, None, None),
        P(users, "items", None, None, None),
        P(users, "items", None),
        P(users, "items", None),
        P(users, "items"),
    )
    return jax.shard_map(
        local, mesh=chips, in_specs=placed, out_specs=P(users, None), check_vma=False
    )
```

time: 1220 us -> 276 us (0.23)
  waiting for transfers between devices: 1100 us -> 109 us
  starting transfers between devices: 0.58 us -> 61.2 us
  matrix products: 42.8 us -> 0.59 us
  blocking collectives: 0 us -> 39 us
  local copies, waits for them, and re-layouts: 48.8 us -> 18.6 us
  Pallas kernels: 0 us -> 27.6 us
    psum x9 -> x0, waiting for transfers between devices: 977 us -> none  [the longest x8 648 us: group_total(): return lax.psum(owner_rows(owners, terms), 'items')]
    all_gather x1 -> x3, waiting for transfers between devices: 126 us -> 15.9 us  [the longest x2 10.3 us: group_blocks(): return lax.all_gather(pick(place, mine, other), 'items', axis=0, tiled=True)]
    all_to_all x0 -> x5, waiting for transfers between devices: none -> 85.9 us  [the longest x3 44.1 us: spread(): return lax.all_to_all(copies, axis, 0, 0)]
    dot_general x25 -> x1, matrix products: 42.8 us -> 0.59 us  [local(): lax.dot_general(line_items[:, :width], line_items, TN, preferred_element_...]
    all_to_all x0 -> x2, blocking collectives: none -> 39 us  [spread(): return lax.all_to_all(copies, axis, 0, 0)]
    all_to_all x0 -> x5, starting transfers between devices: none -> 38.7 us  [the longest x3 26.4 us: spread(): return lax.all_to_all(copies, axis, 0, 0)]
    pallas_call x0 -> x5, Pallas kernels: none -> 27.6 us  [the longest x2 18.4 us: solve(): pl.pallas_call(functools.partial(solve_kernel, block * BLK, implicit, las...]
    ppermute x0 -> x4, starting transfers between devices: none -> 22.4 us  [swap_cores(): return lax.ppermute(value, 'core', [(0, 1), (1, 0)])]
  transfers between devices with their start and end apart: 10 -> 12, of which waited for: 10 -> 10; matrix products, arithmetic and copies ran while one was open for 2% -> 4% of each run, Pallas kernels for 0% -> 7%
where the time goes in v1:
time: 276 us; the launch traced here: 275 us
  waiting for transfers between devices  109 us (39%)
  starting transfers between devices  61.2 us (22%)
  blocking collectives  39 us (14%)
  Pallas kernels  27.6 us (10%)
  local copies, waits for them, and re-layouts  18.6 us (7%)
  between operations  14.1 us (5%)
  other arithmetic  4.6 us (2%)
    all_to_all x3, waiting for transfers between devices, spread(): return lax.all_to_all(copies, axis, 0, 0)  44.1 us
    all_to_all x2, blocking collectives, spread(): return lax.all_to_all(copies, axis, 0, 0)  39 us
    all_to_all x1, waiting for transfers between devices, local(): pack = lax.all_to_all(pack, 'items', 0, 0)  29.6 us
    all_to_all x3, starting transfers between devices, spread(): return lax.all_to_all(copies, axis, 0, 0)  26.4 us
    ppermute x4, starting transfers between devices, swap_cores(): return lax.ppermute(value, 'core', [(0, 1), (1, 0)])  22.4 us
    pallas_call x2, Pallas kernels, solve(): pl.pallas_call(functools.partial(solve_kernel, block * BLK, implicit, las...  18.4 us
    all_to_all x1, waiting for transfers between devices, local(): share = jnp.sum(lax.all_to_all(shares, ('x', 'items'), 0, 0), axis=0)  12.3 us
    all_gather x2, waiting for transfers between devices, group_blocks(): return lax.all_gather(pick(place, mine, other), 'items', axis=0, tiled=True)  10.3 us
  transfers between devices with their start and end apart: 12, of which 10 were waited for; matrix products, arithmetic and copies ran while one was open for 4% of the time, Pallas kernels for 7%

profile of v1, /device:TPU:1, one launch (start us, length us, event | category | flops | bytes accessed | tf_op | source)
XLA Modules:
  0.0 274.9 jit_solution(12485510458671726567)
XLA Ops:
  6.5 0.8 slice.35
  7.3 0.8 broadcast_in_dim.13
  8.1 15.7 %all-to-all-start.2 = ((bf16[12,128,128]{2,1,0:T(8,128)(2,1)}), bf16[12,128,128]{2,1,0:T(8,128)(2,1)S(1)}, u32[]{:S(2)}, u32[]{:S(2)}) async-start(bf16[12,128,128]{2,1,0:T(8,128)(2,1)} %broadcast_in_dim.13), calls=%async_computation.2 | async-start | bytes 786432 | tf_op jit(solution)/shard_map/all_to_all | solution.py:31
  23.8 0.0 all-gather.4.cloned.1.call-start
  23.9 0.7 all-gather.4.cloned.1.call-update
  24.6 0.0 all-gather.6.cloned.1.call-start
  24.6 17.9 %all-to-all-done.2 = bf16[12,128,128]{2,1,0:T(8,128)(2,1)S(1)} async-done(((bf16[12,128,128]{2,1,0:T(8,128)(2,1)}), bf16[12,128,128]{2,1,0:T(8,128)(2,1)S(1)}, u32[]{:S(2)}, u32[]{:S(2)}) %all-to-all-start.2) | async-done | bytes 393248 | tf_op jit(solution)/shard_map/all_to_all | solution.py:31
  42.5 0.4 broadcast_in_dim.14
  42.9 22.2 %all_to_all.35 = bf16[4,12,128,128]{3,2,1,0:T(8,128)(2,1)S(1)} all-to-all(bf16[4,12,128,128]{3,2,1,0:T(8,128)(2,1)S(1)} %broadcast_in_dim.14), channel_id=1, replica_groups=mesh['x'=4,'z'=12,'core'=2,'items'=8] {'x'}, dimensions={0} | all-to-all | bytes 3145728 | tf_op jit(solution)/shard_map/all_to_all | solution.py:31
  65.2 5.1 %collective-permute-start.2 = (bf16[48,128,128]{2,1,0:T(8,128)(2,1)S(1)}, bf16[48,128,128]{2,1,0:T(8,128)(2,1)S(1)}, u32[]{:S(2)}, u32[]{:S(2)}) collective-permute-start(bf16[48,128,128]{2,1,0:T(8,128)(2,1)S(1)} %bitcast.37), channel_id=1, source_target_pairs={{0,8},{8,0},{1,9},{9,1},{2,10},{10,2},{3,11},{11,3},{4,12},{12,4},... | collective-permute-start | bytes 4718600 | tf_op jit(solution)/shard_map/ppermute | solution.py:35
  70.3 0.5 fusion.3.place_ref
  70.9 2.5 collective-permute-done.2.other_ref
  73.3 1.1 copy-done.10
  74.5 2.6 pick.2
  77.1 0.0 all-gather.6.cloned.1.call-update
  77.1 0.0 all-gather.8.cloned.1.call-start
  77.1 5.6 %all-gather.4.cloned.1.call-done = bf16[12,128,512]{2,1,0:T(8,128)(2,1)} async-done(((bf16[1,128,512]{2,1,0:T(8,128)(2,1)}), bf16[12,128,512]{2,1,0:T(8,128)(2,1)}) %all-gather.4.cloned.1.call-update) | async-done | bytes 1572880 | tf_op jit(solution)/shard_map/all_gather | solution.py:241
  82.7 1.0 slice.37
  83.8 0.4 broadcast_in_dim.16
  84.1 16.8 %all_to_all.36 = bf16[4,12,128,128]{3,2,1,0:T(8,128)(2,1)S(1)} all-to-all(bf16[4,12,128,128]{3,2,1,0:T(8,128)(2,1)S(1)} %broadcast_in_dim.16), channel_id=1, replica_groups=mesh['x'=4,'z'=12,'core'=2,'items'=8] {'x'}, dimensions={0} | all-to-all | bytes 3145728 | tf_op jit(solution)/shard_map/all_to_all | solution.py:31
  100.9 10.5 %collective-permute-start.3 = (bf16[48,128,128]{2,1,0:T(8,128)(2,1)S(1)}, bf16[48,128,128]{2,1,0:T(8,128)(2,1)}, u32[]{:S(2)}, u32[]{:S(2)}) collective-permute-start(bf16[48,128,128]{2,1,0:T(8,128)(2,1)S(1)} %bitcast.39), channel_id=1, source_target_pairs={{0,8},{8,0},{1,9},{9,1},{2,10},{10,2},{3,11},{11,3},{4,12},{12,4},... | collective-permute-start | bytes 4718600 | tf_op jit(solution)/shard_map/ppermute | solution.py:35
  111.4 3.1 %collective-permute-done.3.other_ref = bf16[48,128,128]{2,1,0:T(8,128)(2,1)} collective-permute-done((bf16[48,128,128]{2,1,0:T(8,128)(2,1)S(1)}, bf16[48,128,128]{2,1,0:T(8,128)(2,1)}, u32[]{:S(2)}, u32[]{:S(2)}) %collective-permute-start.3) | collective-permute-done | bytes 1572896 | tf_op jit(solution)/shard_map/ppermute | solution.py:35
  114.6 2.6 pick.3
  117.2 0.0 all-gather.8.cloned.1.call-update
  117.2 0.6 fusion
  117.8 0.0 copy-start.15
  117.9 0.0 copy-start.11
  117.9 2.4 collective-permute-start
  120.4 1.1 collective-permute-done
  121.5 0.1 select_add_fusion
  121.6 0.8 reshape.61
  122.4 7.5 %all-to-all-start = ((f32[32,4,512]{2,1,0:T(4,128)}), f32[32,4,512]{2,1,0:T(4,128)S(1)}, u32[]{:S(2)}, u32[]{:S(2)}) async-start(f32[32,4,512]{2,1,0:T(4,128)} %reshape.61), calls=%async_computation | async-start | bytes 524288 | tf_op jit(solution)/shard_map/all_to_all | solution.py:277
  130.5 12.3 %all-to-all-done = f32[32,4,512]{2,1,0:T(4,128)S(1)} async-done(((f32[32,4,512]{2,1,0:T(4,128)}), f32[32,4,512]{2,1,0:T(4,128)S(1)}, u32[]{:S(2)}, u32[]{:S(2)}) %all-to-all-start) | async-done | bytes 262176 | tf_op jit(solution)/shard_map/all_to_all | solution.py:277
  142.8 0.1 reduce_sum.9
  142.9 0.7 broadcast_in_dim.12
  143.6 6.5 %all-to-all-start.1 = ((f32[32,4,512]{2,1,0:T(4,128)}), f32[32,4,512]{2,1,0:T(4,128)S(1)}, u32[]{:S(2)}, u32[]{:S(2)}) async-start(f32[32,4,512]{2,1,0:T(4,128)} %broadcast_in_dim.12), calls=%async_computation.1 | async-start | bytes 524288 | tf_op jit(solution)/shard_map/all_to_all | solution.py:31
  150.1 0.1 copy_bitcast_fusion
  150.2 0.1 broadcast_in_dim.15
  150.3 1.2 pad_maximum_fusion
  151.5 8.2 %all-to-all-done.1 = f32[32,4,512]{2,1,0:T(4,128)S(1)} async-done(((f32[32,4,512]{2,1,0:T(4,128)}), f32[32,4,512]{2,1,0:T(4,128)S(1)}, u32[]{:S(2)}, u32[]{:S(2)}) %all-to-all-start.1) | async-done | bytes 262176 | tf_op jit(solution)/shard_map/all_to_all | solution.py:31
  159.7 4.8 %all-to-all-start.4 = ((bf16[8,33,16,128]{3,2,1,0:T(8,128)(2,1)}), bf16[8,33,16,128]{3,2,1,0:T(8,128)(2,1)S(1)}, u32[]{:S(2)}, u32[]{:S(2)}) async-start(bf16[8,33,16,128]{3,2,1,0:T(8,128)(2,1)} %pad_maximum_fusion), calls=%async_computation.4 | async-start | bytes 2162688 | tf_op jit(solution)/shard_map/all_to_all | solution.py:265
  164.5 0.8 reshape.62
  165.3 4.3 %collective-permute-start.1 = (f32[128,512]{1,0:T(8,128)}, f32[128,512]{1,0:T(8,128)}, u32[]{:S(2)}, u32[]{:S(2)}) collective-permute-start(f32[128,512]{1,0:T(8,128)} %reshape.62), channel_id=1, source_target_pairs={{0,8},{8,0},{1,9},{9,1},{2,10},{10,2},{3,11},{11,3},{4,12},{12,4},... | collective-permute-start | bytes 786440 | tf_op jit(solution)/shard_map/ppermute | solution.py:35
  169.7 0.9 constant_dynamic-slice_fusion
  170.6 29.6 %all-to-all-done.4.pack_ref.side_ref = bf16[8,33,16,128]{3,2,1,0:T(8,128)(2,1)S(1)} async-done(((bf16[8,33,16,128]{3,2,1,0:T(8,128)(2,1)}), bf16[8,33,16,128]{3,2,1,0:T(8,128)(2,1)S(1)}, u32[]{:S(2)}, u32[]{:S(2)}) %all-to-all-start.4) | async-done | bytes 1081376 | tf_op jit(solution)/shard_map/all_to_all | solution.py:265
  200.2 0.2 convert_reduce_fusion
  200.4 0.8 reshape.67.owner_ref
  201.1 0.0 copy-done.1
  201.2 3.9 %widen.1.wide_ref = bf16[128,8192]{1,0:T(8,128)(2,1)} custom-call(s32[128]{0:T(128)} %reshape.67.owner_ref, bf16[8,33,16,128]{3,2,1,0:T(8,128)(2,1)} %copy-done.1), custom_call_target="tpu_custom_call" | custom-call | tf_op jit(solution)/shard_map/widen/pallas_call | solution.py:105
  205.1 1.2 broadcast_select_fusion.1
  206.4 0.0 all-gather.6.cloned.1.call-done.table_ref
  206.4 0.5 copy-done
  206.9 1.2 copy-done.2
  208.1 2.2 copy-done.3
  210.4 9.8 %solve0.1 = (f32[64,512]{1,0:T(8,128)S(1)}, bf16[128,8192]{1,0:T(8,128)(2,1)S(1)}) custom-call(f32[64,512]{1,0:T(8,128)S(1)} %bitcast.36, f32[256,512]{1,0:T(8,128)S(1)} %pad_maximum_fusion.2.gram_ref, bf16[8192,256]{1,0:T(8,128)(2,1)S(1)} %copy-done.3, bf16[128,8192]{1,0:T(8,128)(2,1)S(1)} %copy-done, bf16[8,33,16,128]{3,2,1,0:T(8,128)(2,1)S(1)} %copy-done.2), custom_call_target="tpu_custom_call" | custom-call | tf_op jit(solution)/shard_map/solve0/pallas_call | solution.py:216
  220.1 1.3 copy-done.5
  221.5 10.3 %all-gather.8.cloned.1.call-done.table_ref = bf16[8192,256]{1,0:T(8,128)(2,1)} async-done(((bf16[1024,256]{1,0:T(8,128)(2,1)}), bf16[8192,256]{1,0:T(8,128)(2,1)}) %all-gather.8.cloned.1.call-update) | async-done | bytes 4194320 | tf_op jit(solution)/shard_map/all_gather | solution.py:249
  231.7 2.2 copy-done.4
  233.9 1.6 copy-done.6
  235.5 8.6 %solve1.1 = f32[64,256]{1,0:T(8,128)S(1)} custom-call(f32[64,512]{1,0:T(8,128)S(1)} %get-tuple-element.7.factors_ref, f32[256,512]{1,0:T(8,128)S(1)} %pad_maximum_fusion.2.gram_ref, bf16[8192,256]{1,0:T(8,128)(2,1)S(1)} %copy-done.4, bf16[128,8192]{1,0:T(8,128)(2,1)S(1)} %copy-done, bf16[128,8192]{1,0:T(8,128)(2,1)S(1)} %copy-done.6), custom_call_target="tpu_custom_call" | custom-call | tf_op jit(solution)/shard_map/solve1/pallas_call | solution.py:216
  244.2 0.8 broadcast_in_dim.17
  245.0 4.3 %all-to-all-start.6 = ((f32[8,64,256]{2,1,0:T(8,128)}), f32[8,64,256]{2,1,0:T(8,128)S(1)}, u32[]{:S(2)}, u32[]{:S(2)}) async-start(f32[8,64,256]{2,1,0:T(8,128)} %broadcast_in_dim.17), calls=%async_computation.6 | async-start | bytes 1048576 | tf_op jit(solution)/shard_map/all_to_all | solution.py:31
  249.3 17.9 %all-to-all-done.6 = f32[8,64,256]{2,1,0:T(8,128)S(1)} async-done(((f32[8,64,256]{2,1,0:T(8,128)}), f32[8,64,256]{2,1,0:T(8,128)S(1)}, u32[]{:S(2)}, u32[]{:S(2)}) %all-to-all-start.6) | async-done | bytes 524320 | tf_op jit(solution)/shard_map/all_to_all | solution.py:31
  267.3 1.1 pad_maximum_fusion.1
  (29 shorter events, 0.2 us)
Async XLA Ops:
  8.1 34.4 %all-to-all-start.2 = ((bf16[12,128,128]{2,1,0:T(8,128)(2,1)}), bf16[12,128,128]{2,1,0:T(8,128)(2,1)S(1)}, u32[]{:S(2)}, u32[]{:S(2)}) async-start(bf16[12,128,128]{2,1,0:T(8,128)(2,1)} %broadcast_in_dim.13), calls=%async_computation.2 | async-start | bytes 786432 | tf_op jit(solution)/shard_map/all_to_all | solution.py:31
  23.8 58.9 %all-gather.4.cloned.1.call-start = ((), (), s32[]{:S(2)}) async-start(), calls=%async_computation.7 | async-start | bytes 1703936 | tf_op jit(solution)/shard_map/all_gather | solution.py:241
  24.6 181.9 %all-gather.6.cloned.1.call-start = ((), (), s32[]{:S(2)}) async-start(), calls=%async_computation.8 | async-start | bytes 4718592 | tf_op jit(solution)/shard_map/all_gather | solution.py:249
  42.9 27.4 %copy-start.14 = (s32[1,1,16]{2,1,0:T(1,128)S(1)}, s32[1,1,16]{2,1,0:T(1,128)}, u32[]{:S(2)}) copy-start(s32[1,1,16]{2,1,0:T(1,128)} %param.12) | copy-start | bytes 196
  65.2 8.2 %copy-start.7 = (bf16[4,12,128,128]{3,2,1,0:T(8,128)(2,1)}, bf16[4,12,128,128]{3,2,1,0:T(8,128)(2,1)S(1)}, u32[]{:S(2)}) copy-start(bf16[4,12,128,128]{3,2,1,0:T(8,128)(2,1)S(1)} %all_to_all.35) | copy-start | bytes 4718596
  65.2 8.2 %collective-permute-start.2 = (bf16[48,128,128]{2,1,0:T(8,128)(2,1)S(1)}, bf16[48,128,128]{2,1,0:T(8,128)(2,1)S(1)}, u32[]{:S(2)}, u32[]{:S(2)}) collective-permute-start(bf16[48,128,128]{2,1,0:T(8,128)(2,1)S(1)} %bitcast.37), channel_id=1, source_target_pairs={{0,8},{8,0},{1,9},{9,1},{2,10},{10,2},{3,11},{11,3},{4,12},{12,4},... | collective-permute-start | bytes 4718600 | tf_op jit(solution)/shard_map/ppermute | solution.py:35
  73.3 1.1 copy-start.10
  77.1 154.6 %all-gather.8.cloned.1.call-start = ((), (), s32[]{:S(2)}) async-start(), calls=%async_computation.9 | async-start | bytes 4718592 | tf_op jit(solution)/shard_map/all_gather | solution.py:249
  100.9 13.7 %copy-start.8 = (bf16[4,12,128,128]{3,2,1,0:T(8,128)(2,1)}, bf16[4,12,128,128]{3,2,1,0:T(8,128)(2,1)S(1)}, u32[]{:S(2)}) copy-start(bf16[4,12,128,128]{3,2,1,0:T(8,128)(2,1)S(1)} %all_to_all.36) | copy-start | bytes 4718596
  100.9 16.3 %copy-start.9 = (bf16[12,128,512]{2,1,0:T(8,128)(2,1)S(1)}, bf16[12,128,512]{2,1,0:T(8,128)(2,1)}, u32[]{:S(2)}) copy-start(bf16[12,128,512]{2,1,0:T(8,128)(2,1)} %all-gather.4.cloned.1.call-done) | copy-start | bytes 4718596
  100.9 13.7 %collective-permute-start.3 = (bf16[48,128,128]{2,1,0:T(8,128)(2,1)S(1)}, bf16[48,128,128]{2,1,0:T(8,128)(2,1)}, u32[]{:S(2)}, u32[]{:S(2)}) collective-permute-start(bf16[48,128,128]{2,1,0:T(8,128)(2,1)S(1)} %bitcast.39), channel_id=1, source_target_pairs={{0,8},{8,0},{1,9},{9,1},{2,10},{10,2},{3,11},{11,3},{4,12},{12,4},... | collective-permute-start | bytes 4718600 | tf_op jit(solution)/shard_map/ppermute | solution.py:35
  117.8 12.6 %copy-start.15 = (s32[1,1,16]{2,1,0:T(1,128)S(1)}, s32[1,1,16]{2,1,0:T(1,128)}, u32[]{:S(2)}) copy-start(s32[1,1,16]{2,1,0:T(1,128)} %param.11) | copy-start | bytes 196
  117.9 32.2 %copy-start.11 = (bf16[1,1,16,128,128]{4,3,2,1,0:T(8,128)(2,1)S(1)}, bf16[1,1,16,128,128]{4,3,2,1,0:T(8,128)(2,1)}, u32[]{:S(2)}) copy-start(bf16[1,1,16,128,128]{4,3,2,1,0:T(8,128)(2,1)} %param.10) | copy-start | bytes 1572868
  117.9 32.2 %copy-start.12 = (bf16[1,1,16,128,128]{4,3,2,1,0:T(8,128)(2,1)S(1)}, bf16[1,1,16,128,128]{4,3,2,1,0:T(8,128)(2,1)}, u32[]{:S(2)}) copy-start(bf16[1,1,16,128,128]{4,3,2,1,0:T(8,128)(2,1)} %param.9) | copy-start | bytes 1572868
  117.9 3.6 %collective-permute-start = (f32[128,512]{1,0:T(8,128)S(1)}, f32[128,512]{1,0:T(8,128)S(1)}, u32[]{:S(2)}, u32[]{:S(2)}) collective-permute-start(f32[128,512]{1,0:T(8,128)S(1)} %slice_select_fusion), channel_id=1, source_target_pairs={{0,8},{8,0},{1,9},{9,1},{2,10},{10,2},{3,11},{11,3},{4,12},{12,4},... | collective-permute-start | bytes 786440 | tf_op jit(solution)/shard_map/ppermute | solution.py:35
  122.4 20.4 %all-to-all-start = ((f32[32,4,512]{2,1,0:T(4,128)}), f32[32,4,512]{2,1,0:T(4,128)S(1)}, u32[]{:S(2)}, u32[]{:S(2)}) async-start(f32[32,4,512]{2,1,0:T(4,128)} %reshape.61), calls=%async_computation | async-start | bytes 524288 | tf_op jit(solution)/shard_map/all_to_all | solution.py:277
  143.6 16.1 %all-to-all-start.1 = ((f32[32,4,512]{2,1,0:T(4,128)}), f32[32,4,512]{2,1,0:T(4,128)S(1)}, u32[]{:S(2)}, u32[]{:S(2)}) async-start(f32[32,4,512]{2,1,0:T(4,128)} %broadcast_in_dim.12), calls=%async_computation.1 | async-start | bytes 524288 | tf_op jit(solution)/shard_map/all_to_all | solution.py:31
  159.7 40.5 %all-to-all-start.4 = ((bf16[8,33,16,128]{3,2,1,0:T(8,128)(2,1)}), bf16[8,33,16,128]{3,2,1,0:T(8,128)(2,1)S(1)}, u32[]{:S(2)}, u32[]{:S(2)}) async-start(bf16[8,33,16,128]{3,2,1,0:T(8,128)(2,1)} %pad_maximum_fusion), calls=%async_computation.4 | async-start | bytes 2162688 | tf_op jit(solution)/shard_map/all_to_all | solution.py:265
  165.3 39.8 %collective-permute-start.1 = (f32[128,512]{1,0:T(8,128)}, f32[128,512]{1,0:T(8,128)}, u32[]{:S(2)}, u32[]{:S(2)}) collective-permute-start(f32[128,512]{1,0:T(8,128)} %reshape.62), channel_id=1, source_target_pairs={{0,8},{8,0},{1,9},{9,1},{2,10},{10,2},{3,11},{11,3},{4,12},{12,4},... | collective-permute-start | bytes 786440 | tf_op jit(solution)/shard_map/ppermute | solution.py:35
  200.2 1.0 copy-start.1
  205.1 1.8 copy-start
  206.9 1.2 copy-start.2
  208.1 2.2 copy-start.3
  220.1 1.3 copy-start.5
  231.7 2.2 copy-start.4
  233.9 1.6 copy-start.6
  244.2 5.1 %copy-start.13 = (f32[512,512]{1,0:T(8,128)S(1)}, f32[512,512]{1,0:T(8,128)}, u32[]{:S(2)}) copy-start(f32[512,512]{1,0:T(8,128)} %param.7) | copy-start | bytes 3145732
  245.0 22.2 %all-to-all-start.6 = ((f32[8,64,256]{2,1,0:T(8,128)}), f32[8,64,256]{2,1,0:T(8,128)S(1)}, u32[]{:S(2)}, u32[]{:S(2)}) async-start(f32[8,64,256]{2,1,0:T(8,128)} %broadcast_in_dim.17), calls=%async_computation.6 | async-start | bytes 1048576 | tf_op jit(solution)/shard_map/all_to_all | solution.py:31
Sparse Core Ops, SparseCore 0:
  27.1 55.6 all-gather.3
  85.1 68.7 all-gather.5
  156.3 75.3 all-gather.7

commit v2 on v1

--- a/solution.py
+++ b/solution.py
@@ -35,30 +35,21 @@
     return lax.ppermute(value, "core", [(0, 1), (1, 0)])
 
 
-def pick_kernel(place_ref, mine_ref, other_ref, out_ref, sems):
+def pick_kernel(place_ref, mine_ref, other_ref, out_ref):
     tiles = place_ref.shape[0]
     per_core = mine_ref.shape[0]
 
-    def copy(source, row, t):
-        return pltpu.make_async_copy(
-            source.at[row],
-            out_ref.at[pl.ds((t // 2) * BLK, BLK), pl.ds((t % 2) * BLK, BLK)],
-            sems.at[t],
-        )
-
     for t in range(tiles):
         place = place_ref[t]
+        at = (pl.ds((t // 2) * BLK, BLK), pl.ds((t % 2) * BLK, BLK))
 
         @pl.when(place < per_core)
         def _():
-            copy(mine_ref, place, t).start()
+            out_ref[at] = mine_ref[place]
 
         @pl.when(place >= per_core)
         def _():
-            copy(other_ref, place - per_core, t).start()
-
-    for t in range(tiles):
-        copy(mine_ref, 0, t).wait()
+            out_ref[at] = other_ref[place - per_core]
 
 
 def pick(place, mine, other):
@@ -68,11 +59,11 @@
         out_shape=jax.ShapeDtypeStruct((tiles // 2 * BLK, 2 * BLK), jnp.bfloat16),
         in_specs=[
             pl.BlockSpec(memory_space=pltpu.SMEM),
-            pl.BlockSpec(memory_space=pl.ANY),
-            pl.BlockSpec(memory_space=pl.ANY),
+            pl.BlockSpec(memory_space=pltpu.VMEM),
+            pl.BlockSpec(memory_space=pltpu.VMEM),
         ],
         out_specs=pl.BlockSpec(memory_space=pltpu.VMEM),
-        scratch_shapes=[pltpu.SemaphoreType.DMA((tiles,))],
+        compiler_params=pltpu.CompilerParams(vmem_limit_bytes=16 * 1024 * 1024),
         name="pick",
     )(place, mine, other)
 
@@ -121,21 +112,44 @@
 
 
 def solve_kernel(
-    low, implicit, last, factors_ref, gram_ref, table_ref, wide_ref, side_ref, *rest
+    low, implicit, last, factors_hbm, gram_hbm, table_hbm, wide_hbm, side_hbm, *rest
 ):
     if last:
-        (out_ref,) = rest
+        news_ref, *held = rest
     else:
-        out_ref, errors_ref = rest
+        news_ref, factors_out, errors_ref, *held = rest
+    factors_ref, gram_ref, table_ref, wide_ref, side_ref, flip_ref, whole_sems, sems = held
     users = factors_ref.shape[0]
     rows, columns = wide_ref.shape
-    width = 1024
+    width = columns // sems.shape[1]
     chunks = columns // width
     tiles = width // BLK
 
+    def load(part, c):
+        at = pl.ds(c * width, width)
+        source, target = ((table_hbm, table_ref), (side_hbm, side_ref), (wide_hbm, wide_ref))[part]
+        if part == 0:
+            source, target = source.at[at], target.at[at]
+        elif part == 1 and low == 0:
+            source, target = source.at[c], target.at[c]
+        else:
+            source, target = source.at[:, at], target.at[:, at]
+        return pltpu.make_async_copy(source, target, sems.at[part, c])
+
+    load_factors = pltpu.make_async_copy(factors_hbm, factors_ref, whole_sems.at[0])
+    load_gram = pltpu.make_async_copy(gram_hbm, gram_ref, whole_sems.at[1])
+    load_factors.start()
+    load_gram.start()
+    for c in range(chunks):
+        for part in range(3 if low == 0 else 2):
+            load(part, c).start()
+    if low:
+        for c in range(chunks):
+            load(2, c).start()
+
     def pieces(c):
         at = pl.ds(c * width, width)
-        return table_ref[at, :], wide_ref[:, at].astype(jnp.float32)
+        return table_ref[at, :], flip_ref[:, at], wide_ref[:, at].astype(jnp.float32)
 
     def scores(c):
         parts = []
@@ -158,26 +172,40 @@
         both = pair_rows(direction)
         total = jnp.zeros((rows, 2 * BLK), jnp.float32)
         for c in range(chunks):
-            table, weights = pieces(c)
-            seen = lax.dot_general(both, table, NT, preferred_element_type=jnp.float32)
+            table, flip, weights = pieces(c)
+            seen = lax.dot_general(both, flip, NN, preferred_element_type=jnp.float32)
             scaled = (seen * weights).astype(jnp.bfloat16)
             total += lax.dot_general(scaled, table, NN, preferred_element_type=jnp.float32)
         return fold(total)
 
+    load_factors.wait()
+    load_gram.wait()
+    factors = factors_ref[...]
+    current = factors[:, low : low + BLK]
+    gram_columns = gram_ref[...]
+    gram_diag = gram_columns[low : low + BLK, :]
+    local_grad = implicit * exact_dot(factors, gram_columns, NN) + ridge_weight * current
+
     total = jnp.zeros((rows, 2 * BLK), jnp.float32)
     for c in range(chunks):
-        table, weights = pieces(c)
+        for part in range(3 if low == 0 else 2):
+            load(part, c).wait()
+        at = pl.ds(c * width, width)
+        flip_ref[:, at] = table_ref[at, :].T
         if low == 0:
+            table, _, weights = pieces(c)
             errors = ((scores(c) - 1.0) * weights).astype(jnp.bfloat16)
         else:
-            errors = side_ref[:, pl.ds(c * width, width)]
+            at = pl.ds(c * width, width)
+            table = table_ref[at, :]
+            errors = side_ref[:, at]
         total += lax.dot_general(errors, table, NN, preferred_element_type=jnp.float32)
 
-    factors = factors_ref[...]
-    current = factors[:, low : low + BLK]
-    gram_rows = gram_ref[low : low + BLK, :]
-    gram_diag = gram_rows[:, low : low + BLK]
-    grad = implicit * exact_dot(factors, gram_rows, NT) + ridge_weight * current + fold(total)
+    if low:
+        for c in range(chunks):
+            load(2, c).wait()
+
+    grad = local_grad + fold(total)
     resid = -grad
     direction = resid
     delta = jnp.zeros_like(resid)
@@ -192,35 +220,43 @@
             norm_next = jnp.sum(resid * resid, axis=1, keepdims=True)
             direction = resid + norm_next / norm_now * direction
             norm_now = norm_next
-    if low:
-        out_ref[:, :low] = factors[:, :low]
-    out_ref[:, low : low + BLK] = current + delta
+    new = current + delta
+    for copy in range(news_ref.shape[0]):
+        news_ref[copy] = new
     if last:
         return
-    out_ref[:, low + BLK :] = factors[:, low + BLK :]
+    if low:
+        factors_out[:, :low] = factors[:, :low]
+    factors_out[:, low : low + BLK] = new
+    factors_out[:, low + BLK :] = factors[:, low + BLK :]
     both = pair_rows(delta)
     for c in range(chunks):
-        table, weights = pieces(c)
-        seen = lax.dot_general(both, table, NT, preferred_element_type=jnp.float32)
+        table, flip, weights = pieces(c)
+        seen = lax.dot_general(both, flip, NN, preferred_element_type=jnp.float32)
         predicted = scores(c) + seen
         errors_ref[:, pl.ds(c * width, width)] = ((predicted - 1.0) * weights).astype(jnp.bfloat16)
 
 
-def solve(block, implicit, factors, gram, table, wide, side):
+def solve(block, implicit, copies, factors, gram, table, wide, side):
     last = block + 1 == SWEEP
     users = factors.shape[0]
-    out_width = SWEEP * BLK if last else D
-    shapes = [jax.ShapeDtypeStruct((users, out_width), jnp.float32)]
+    shapes = [jax.ShapeDtypeStruct((copies, users, BLK), jnp.float32)]
     if not last:
+        shapes.append(jax.ShapeDtypeStruct((users, D), jnp.float32))
         shapes.append(jax.ShapeDtypeStruct(wide.shape, jnp.bfloat16))
+    operands = (factors, gram, table, wide, side)
+    chunks = copies
     return pl.pallas_call(
         functools.partial(solve_kernel, block * BLK, implicit, last),
         out_shape=shapes,
-        in_specs=[pl.BlockSpec(memory_space=pltpu.VMEM)] * 5,
+        in_specs=[pl.BlockSpec(memory_space=pl.ANY)] * len(operands),
         out_specs=[pl.BlockSpec(memory_space=pltpu.VMEM)] * len(shapes),
-        compiler_params=pltpu.CompilerParams(vmem_limit_bytes=40 * 1024 * 1024),
+        scratch_shapes=[pltpu.VMEM(value.shape, value.dtype) for value in operands]
+        + [pltpu.VMEM(table.shape[::-1], table.dtype)]
+        + [pltpu.SemaphoreType.DMA((2,)), pltpu.SemaphoreType.DMA((3, chunks))],
+        compiler_params=pltpu.CompilerParams(vmem_limit_bytes=56 * 1024 * 1024),
         name="solve%d" % block,
-    )(factors, gram, table, wide, side)
+    )(*operands)
 
 
 def local(
@@ -237,19 +273,10 @@
     core = lax.axis_index("core")
     group = lax.axis_index("items")
     own_items = item_factors[0]
-
-    line = lax.all_gather(own_items, "z", axis=0)
-    item_idx = tile_items[0, 0]
-    chip_block = item_idx // CORES
-    place = chip_block + (item_idx % CORES != core).astype(jnp.int32) * (n_x * n_z)
-
-    def group_blocks(line_columns):
-        mine = spread(line_columns, "x").reshape(n_x * n_z, BLK, BLK)
-        other = swap_cores(mine)
-        return lax.all_gather(pick(place, mine, other), "items", axis=0, tiled=True)
-
-    table0 = group_blocks(spread(own_items[:, :BLK], "z"))
-    table1 = group_blocks(line[:, :, BLK:width])
+    at_x = lax.axis_index("x")
+
+    def along_x(value, shift):
+        return lax.ppermute(value, "x", [(i, (i + shift) % n_x) for i in range(n_x)])
 
     live = jnp.arange(tiles) < tile_count[0, 0]
     live_weights = tile_weights[0, 0] * live[:, None, None].astype(jnp.bfloat16)
@@ -262,33 +289,74 @@
         return value.reshape(tiles, n_items, own, BLK).transpose(1, 0, 2, 3)
 
     pack = jnp.concatenate([by_user(live_weights), by_user(tile_scores[0, 0]), owner_rows], axis=1)
+    pack = pack.reshape(n_items, -1, BLK)
+
+    partial = lax.dot_general(
+        own_items, own_items[:, :width], TN, preferred_element_type=jnp.float32
+    )
+    half = jnp.where(core == 0, partial[:, :BLK], partial[:, BLK:])
+    half = half + swap_cores(jnp.where(core == 0, partial[:, BLK:], partial[:, :BLK]))
+    parts = half.reshape(n_x, -1, BLK)
+
+    item_idx = tile_items[0, 0]
+    chip = item_idx // CORES
+    behind = (at_x - chip // n_z) % n_x
+    place = behind * n_z + chip % n_z
+    place = place + (item_idx % CORES != core).astype(jnp.int32) * (n_x * n_z)
+
+    def round_x(blocks):
+        middle = blocks.shape[0] // 2
+        behind = along_x(blocks, 1)
+        ahead = along_x(blocks, -1)
+        opposite = [along_x(behind[:middle], 1), along_x(ahead[middle:], -1)]
+        return jnp.concatenate([blocks, behind, *opposite, ahead], axis=0)
+
+    line0 = spread(own_items[:, :BLK], "z")
+    line0, parts, pack = lax.optimization_barrier((line0, parts, pack))
+    mine0 = round_x(line0)
     pack = lax.all_to_all(pack, "items", 0, 0)
+    picked0 = pick(place, mine0, swap_cores(mine0))
+    picked0, pack = lax.optimization_barrier((picked0, pack))
+    table0 = lax.all_gather(picked0, "items", axis=0, tiled=True)
+
+    columns1, _, pack = lax.optimization_barrier((own_items[:, BLK:width], picked0, pack))
+    line1 = spread(columns1, "z")
+    parts, _ = lax.optimization_barrier((parts, picked0))
+    share = lax.dynamic_index_in_dim(parts, at_x, axis=0, keepdims=False)
+    for shift in range(1, n_x):
+        part = lax.dynamic_index_in_dim(parts, (at_x + shift) % n_x, axis=0, keepdims=False)
+        share = share + along_x(part, shift)
+    line1, share = lax.optimization_barrier((line1, share))
+    mine1 = round_x(line1)
+    share = jnp.sum(lax.all_to_all(share.reshape(n_items, -1, BLK), "items", 0, 0), axis=0)
+    mine1, share = lax.optimization_barrier((mine1, share))
+    picked1 = pick(place, mine1, swap_cores(mine1))
+    table1 = lax.all_gather(picked1, "items", axis=0, tiled=True)
+
+    pack = pack.reshape(n_items, -1, own, BLK)
     owner = pack[:, 2 * tiles, :tiles, 0].astype(jnp.int32).reshape(-1)
     wide = widen(owner, pack)
 
-    line_items = line.reshape(n_z * BLK, D)
-    partial = lax.dot_general(
-        line_items[:, :width], line_items, TN, preferred_element_type=jnp.float32
-    ).reshape(CORES, BLK, D)
-    half = jnp.where(core == 0, partial[0], partial[1])
-    send = jnp.where(core == 0, partial[1], partial[0])
-    half = half + swap_cores(send)
-    shares = half.reshape(n_x * n_items, -1, D)
-    share = jnp.sum(lax.all_to_all(shares, ("x", "items"), 0, 0), axis=0)
-    half = spread(share, ("x", "items")).reshape(BLK, D)
-    there = swap_cores(half)
-    gram = jnp.concatenate(
-        [jnp.where(core == 0, half, there), jnp.where(core == 0, there, half)], axis=0
-    )
+    share = jnp.sum(spread(share, "z"), axis=0)
+    share, wide = lax.optimization_barrier((share, wide))
+    share = spread(share, "items").reshape(-1, BLK)
+    gram = spread(share, ("x", "core")).reshape(n_x, CORES, -1, BLK)
+    gram0 = gram[:, 0].reshape(D, BLK)
+    gram1 = gram[:, 1].reshape(D, BLK)
 
     factors = lax.dynamic_index_in_dim(
         user_factors.reshape(UB_DEV, n_items, own, D), group, axis=1, keepdims=False
     ).reshape(UB_DEV * own, D)
-    factors, errors = solve(0, implicit, factors, gram, table0, wide, pack)
-    (swept,) = solve(1, implicit, factors, gram, table1, wide, errors)
-    swept = spread(swept, "items").reshape(n_items, UB_DEV, own, width)
-    swept = swept.transpose(1, 0, 2, 3).reshape(-1, width)
-    return jnp.concatenate([swept, user_factors[:, width:]], axis=1)
+
+    def all_users(news):
+        news = lax.all_to_all(news, "items", 0, 0).reshape(n_items, UB_DEV, own, BLK)
+        return news.transpose(1, 0, 2, 3).reshape(-1, BLK)
+
+    news0, factors, errors = solve(0, implicit, n_items, factors, gram0, table0, wide, pack)
+    (news1,) = solve(1, implicit, n_items, factors, gram1, table1, wide, errors)
+    return jnp.concatenate(
+        [all_users(news0), all_users(news1), user_factors[:, width:]], axis=1
+    )
 
 
 def solution(mesh):

time: 276 us -> 244 us (0.88)
  starting transfers between devices: 61.2 us -> 100 us
  waiting for transfers between devices: 109 us -> 72 us
  blocking collectives: 39 us -> 10.3 us
  local copies, waits for them, and re-layouts: 18.6 us -> 8.48 us
  Pallas kernels: 27.6 us -> 31.8 us
    ppermute x0 -> x11, starting transfers between devices: none -> 31.5 us  [along_x(): lax.ppermute(value, 'x', [(i, (i + shift) % n_x) for i in range(n_x)])]
    all_to_all x2 -> x1, blocking collectives: 39 us -> 10.3 us  [spread(): return lax.all_to_all(copies, axis, 0, 0)]
    all_to_all x1, waiting for transfers between devices: 29.6 us -> 8.02 us  [local(): pack = lax.all_to_all(pack, 'items', 0, 0)]
    all_gather x3 -> x2, waiting for transfers between devices: 15.9 us -> 0.02 us  [the longest x1 0.02 us: local(): table1 = lax.all_gather(picked1, 'items', axis=0, tiled=True)]
    all_to_all x3 -> x4, waiting for transfers between devices: 44.1 us -> 30.7 us  [spread(): return lax.all_to_all(copies, axis, 0, 0)]
    ppermute x0 -> x11, waiting for transfers between devices: none -> 13.2 us  [along_x(): lax.ppermute(value, 'x', [(i, (i + shift) % n_x) for i in range(n_x)])]
    unnamed x32 -> x22, local copies, waits for them, and re-layouts: 10.2 us -> 0.3 us
    ppermute x4 -> x3, starting transfers between devices: 22.4 us -> 15.3 us  [swap_cores(): return lax.ppermute(value, 'core', [(0, 1), (1, 0)])]
  transfers between devices with their start and end apart: 12 -> 24, of which waited for: 10 -> 15; matrix products, arithmetic and copies ran while one was open for 4% -> 4% of each run, Pallas kernels for 7% -> 13%
where the time goes in v2:
time: 244 us; the launch traced here: 242 us
  starting transfers between devices  100 us (41%)
  waiting for transfers between devices  72 us (30%)
  Pallas kernels  31.8 us (13%)
  between operations  14.6 us (6%)
  blocking collectives  10.3 us (4%)
  local copies, waits for them, and re-layouts  8.48 us (3%)
  other arithmetic  3.8 us (2%)
    all_to_all x4, starting transfers between devices, spread(): return lax.all_to_all(copies, axis, 0, 0)  33 us
    ppermute x11, starting transfers between devices, along_x(): lax.ppermute(value, 'x', [(i, (i + shift) % n_x) for i in range(n_x)])  31.5 us
    all_to_all x4, waiting for transfers between devices, spread(): return lax.all_to_all(copies, axis, 0, 0)  30.7 us
    pallas_call x2, Pallas kernels, solve(): pl.pallas_call(functools.partial(solve_kernel, block * BLK, implicit, las...  24.8 us
    ppermute x3, starting transfers between devices, swap_cores(): return lax.ppermute(value, 'core', [(0, 1), (1, 0)])  15.3 us
    ppermute x11, waiting for transfers between devices, along_x(): lax.ppermute(value, 'x', [(i, (i + shift) % n_x) for i in range(n_x)])  13.2 us
    all_to_all x1, blocking collectives, spread(): return lax.all_to_all(copies, axis, 0, 0)  10.3 us
    all_to_all x2, waiting for transfers between devices, all_users(): lax.all_to_all(news, 'items', 0, 0).reshape(n_items, UB_DEV, own, BLK)  10 us
  transfers between devices with their start and end apart: 24, of which 15 were waited for; matrix products, arithmetic and copies ran while one was open for 4% of the time, Pallas kernels for 13%

profile of v2, /device:TPU:1, one launch (start us, length us, event | category | flops | bytes accessed | tf_op | source)
XLA Modules:
  0.0 242.1 jit_solution(8269436589504905529)
XLA Ops:
  6.5 1.5 fusion.9
  8.0 0.8 broadcast_in_dim.14
  8.8 15.8 %all-to-all-start = ((bf16[12,128,128]{2,1,0:T(8,128)(2,1)}), bf16[12,128,128]{2,1,0:T(8,128)(2,1)S(1)}, u32[]{:S(2)}, u32[]{:S(2)}) async-start(bf16[12,128,128]{2,1,0:T(8,128)(2,1)} %broadcast_in_dim.14), calls=%async_computation | async-start | bytes 786432 | tf_op jit(solution)/shard_map/all_to_all | solution.py:31
  24.7 1.2 fusion
  25.9 2.9 %collective-permute-start = (f32[512,128]{1,0:T(8,128)S(1)}, f32[512,128]{1,0:T(8,128)S(1)}, u32[]{:S(2)}, u32[]{:S(2)}) collective-permute-start(f32[512,128]{1,0:T(8,128)S(1)} %slice_select_fusion), channel_id=1, source_target_pairs={{0,8},{8,0},{1,9},{9,1},{2,10},{10,2},{3,11},{11,3},{4,12},{12,4},... | collective-permute-start | bytes 786440 | tf_op jit(solution)/shard_map/ppermute | solution.py:35
  29.4 0.1 multiply_bitcast_fusion
  29.5 0.1 broadcast_in_dim.15
  29.6 0.1 pad_maximum_fusion
  29.8 1.2 copy.17
  30.9 0.8 select_add_fusion
  31.7 11.6 %all-to-all-done = bf16[12,128,128]{2,1,0:T(8,128)(2,1)S(1)} async-done(((bf16[12,128,128]{2,1,0:T(8,128)(2,1)}), bf16[12,128,128]{2,1,0:T(8,128)(2,1)S(1)}, u32[]{:S(2)}, u32[]{:S(2)}) %all-to-all-start) | async-done | bytes 393248 | tf_op jit(solution)/shard_map/all_to_all | solution.py:31
  43.3 3.1 %collective-permute-start.1 = (bf16[12,128,128]{2,1,0:T(8,128)(2,1)S(1)}, bf16[12,128,128]{2,1,0:T(8,128)(2,1)S(1)}, u32[]{:S(2)}, u32[]{:S(2)}) collective-permute-start(bf16[12,128,128]{2,1,0:T(8,128)(2,1)S(1)} %all-to-all-done), channel_id=1, source_target_pairs={{0,192},{192,384},{384,576},{576,0},{1,193},{193,385},{385,577},{5... | collective-permute-start | bytes 1179656 | tf_op jit(solution)/shard_map/ppermute | solution.py:279
  46.5 3.4 %collective-permute-start.3 = (bf16[12,128,128]{2,1,0:T(8,128)(2,1)S(1)}, bf16[12,128,128]{2,1,0:T(8,128)(2,1)S(1)}, u32[]{:S(2)}, u32[]{:S(2)}) collective-permute-start(bf16[12,128,128]{2,1,0:T(8,128)(2,1)S(1)} %all-to-all-done), channel_id=1, source_target_pairs={{0,576},{192,0},{384,192},{576,384},{1,577},{193,1},{385,193},{577... | collective-permute-start | bytes 1179656 | tf_op jit(solution)/shard_map/ppermute | solution.py:279
  49.8 6.8 %all-to-all-start.1 = ((bf16[8,528,128]{2,1,0:T(8,128)(2,1)}), bf16[8,528,128]{2,1,0:T(8,128)(2,1)}, u32[]{:S(2)}, u32[]{:S(2)}) async-start(bf16[8,528,128]{2,1,0:T(8,128)(2,1)} %bitcast.11), calls=%async_computation.1 | async-start | bytes 2162688 | tf_op jit(solution)/shard_map/all_to_all | solution.py:317
  56.8 1.9 collective-permute-start.2
  58.8 4.6 %collective-permute-start.4 = (bf16[6,128,128]{2,1,0:T(8,128)(2,1)S(1)}, bf16[6,128,128]{2,1,0:T(8,128)(2,1)S(1)}, u32[]{:S(2)}, u32[]{:S(2)}) collective-permute-start(bf16[6,128,128]{2,1,0:T(8,128)(2,1)S(1)} %slice.60), channel_id=1, source_target_pairs={{0,576},{192,0},{384,192},{576,384},{1,577},{193,1},{385,193},{577... | collective-permute-start | bytes 589832 | tf_op jit(solution)/shard_map/ppermute | solution.py:279
  63.3 0.1 constant_dynamic-update-slice_fusion.3
  63.4 1.0 collective-permute-done.2
  64.4 1.5 collective-permute-done.4
  66.0 0.1 constant_dynamic-update-slice_fusion.mine_ref
  66.0 5.9 %collective-permute-start.5 = (bf16[48,128,128]{2,1,0:T(8,128)(2,1)S(1)}, bf16[48,128,128]{2,1,0:T(8,128)(2,1)S(1)}, u32[]{:S(2)}, u32[]{:S(2)}) collective-permute-start(bf16[48,128,128]{2,1,0:T(8,128)(2,1)S(1)} %constant_dynamic-update-slice_fusion.mine_ref), channel_id=1, source_target_pairs={{0,8},{8,0},{1,9},{9,1},{2,10},{10,2},{3,11},{11,3},{4,12},{12,4},... | collective-permute-start | bytes 4718600 | tf_op jit(solution)/shard_map/ppermute | solution.py:35
  72.0 3.0 %collective-permute-done.5.other_ref = bf16[48,128,128]{2,1,0:T(8,128)(2,1)S(1)} collective-permute-done((bf16[48,128,128]{2,1,0:T(8,128)(2,1)S(1)}, bf16[48,128,128]{2,1,0:T(8,128)(2,1)S(1)}, u32[]{:S(2)}, u32[]{:S(2)}) %collective-permute-start.5) | collective-permute-done | bytes 1572896 | tf_op jit(solution)/shard_map/ppermute | solution.py:35
  75.0 1.6 pick.2
  76.6 8.0 %all-to-all-done.1 = bf16[8,528,128]{2,1,0:T(8,128)(2,1)} async-done(((bf16[8,528,128]{2,1,0:T(8,128)(2,1)}), bf16[8,528,128]{2,1,0:T(8,128)(2,1)}, u32[]{:S(2)}, u32[]{:S(2)}) %all-to-all-start.1) | async-done | bytes 1081376 | tf_op jit(solution)/shard_map/all_to_all | solution.py:317
  84.6 0.8 broadcast_in_dim.16
  85.4 6.6 %all-to-all-start.2 = ((bf16[12,128,128]{2,1,0:T(8,128)(2,1)}), bf16[12,128,128]{2,1,0:T(8,128)(2,1)S(1)}, u32[]{:S(2)}, u32[]{:S(2)}) async-start(bf16[12,128,128]{2,1,0:T(8,128)(2,1)} %broadcast_in_dim.16), calls=%async_computation.2 | async-start | bytes 786432 | tf_op jit(solution)/shard_map/all_to_all | solution.py:31
  92.2 3.2 %collective-permute-start.8 = (f32[128,128]{1,0:T(8,128)S(1)}, f32[128,128]{1,0:T(8,128)S(1)}, u32[]{:S(2)}, u32[]{:S(2)}) collective-permute-start(f32[128,128]{1,0:T(8,128)S(1)} %get-tuple-element.42), channel_id=1, source_target_pairs={{0,576},{192,0},{384,192},{576,384},{1,577},{193,1},{385,193},{577... | collective-permute-start | bytes 196616 | tf_op jit(solution)/shard_map/ppermute | solution.py:279
  95.4 2.4 %collective-permute-start.7 = (f32[128,128]{1,0:T(8,128)S(1)}, f32[128,128]{1,0:T(8,128)S(1)}, u32[]{:S(2)}, u32[]{:S(2)}) collective-permute-start(f32[128,128]{1,0:T(8,128)S(1)} %get-tuple-element.43), channel_id=1, source_target_pairs={{0,384},{192,576},{384,0},{576,192},{1,385},{193,577},{385,1},{577... | collective-permute-start | bytes 196616 | tf_op jit(solution)/shard_map/ppermute | solution.py:279
  97.8 2.5 %collective-permute-start.6 = (f32[128,128]{1,0:T(8,128)S(1)}, f32[128,128]{1,0:T(8,128)S(1)}, u32[]{:S(2)}, u32[]{:S(2)}) collective-permute-start(f32[128,128]{1,0:T(8,128)S(1)} %get-tuple-element.41), channel_id=1, source_target_pairs={{0,192},{192,384},{384,576},{576,0},{1,193},{193,385},{385,577},{5... | collective-permute-start | bytes 196616 | tf_op jit(solution)/shard_map/ppermute | solution.py:279
  100.3 1.8 collective-permute-done.7
  102.2 2.3 collective-permute-done.6
  104.5 0.6 fusion.3
  105.1 5.5 %all-to-all-done.2 = bf16[12,128,128]{2,1,0:T(8,128)(2,1)S(1)} async-done(((bf16[12,128,128]{2,1,0:T(8,128)(2,1)}), bf16[12,128,128]{2,1,0:T(8,128)(2,1)S(1)}, u32[]{:S(2)}, u32[]{:S(2)}) %all-to-all-start.2) | async-done | bytes 393248 | tf_op jit(solution)/shard_map/all_to_all | solution.py:31
  110.7 1.9 collective-permute-start.9
  112.6 4.6 %collective-permute-start.11 = (bf16[12,128,128]{2,1,0:T(8,128)(2,1)S(1)}, bf16[12,128,128]{2,1,0:T(8,128)(2,1)S(1)}, u32[]{:S(2)}, u32[]{:S(2)}) collective-permute-start(bf16[12,128,128]{2,1,0:T(8,128)(2,1)S(1)} %all-to-all-done.2), channel_id=1, source_target_pairs={{0,576},{192,0},{384,192},{576,384},{1,577},{193,1},{385,193},{577... | collective-permute-start | bytes 1179656 | tf_op jit(solution)/shard_map/ppermute | solution.py:279
  117.2 3.4 %all-to-all-start.3 = ((f32[8,16,128]{2,1,0:T(8,128)}), f32[8,16,128]{2,1,0:T(8,128)S(1)}, u32[]{:S(2)}, u32[]{:S(2)}) async-start(f32[8,16,128]{2,1,0:T(8,128)} %bitcast.16), calls=%async_computation.3 | async-start | bytes 131072 | tf_op jit(solution)/shard_map/all_to_all | solution.py:331
  120.6 1.8 collective-permute-done.9
  122.4 1.9 collective-permute-start.10
  124.3 4.0 %all-to-all-done.3 = f32[8,16,128]{2,1,0:T(8,128)S(1)} async-done(((f32[8,16,128]{2,1,0:T(8,128)}), f32[8,16,128]{2,1,0:T(8,128)S(1)}, u32[]{:S(2)}, u32[]{:S(2)}) %all-to-all-start.3) | async-done | bytes 65568 | tf_op jit(solution)/shard_map/all_to_all | solution.py:331
  128.4 2.0 collective-permute-start.12
  130.4 0.1 constant_dynamic-update-slice_fusion.8
  130.5 4.7 %collective-permute-done.12 = bf16[6,128,128]{2,1,0:T(8,128)(2,1)S(1)} collective-permute-done((bf16[6,128,128]{2,1,0:T(8,128)(2,1)S(1)}, bf16[6,128,128]{2,1,0:T(8,128)(2,1)S(1)}, u32[]{:S(2)}, u32[]{:S(2)}) %collective-permute-start.12) | collective-permute-done | bytes 196640 | tf_op jit(solution)/shard_map/ppermute | solution.py:279
  135.2 0.1 constant_dynamic-update-slice_fusion.5.mine_ref
  135.3 6.5 %collective-permute-start.13 = (bf16[48,128,128]{2,1,0:T(8,128)(2,1)S(1)}, bf16[48,128,128]{2,1,0:T(8,128)(2,1)S(1)}, u32[]{:S(2)}, u32[]{:S(2)}) collective-permute-start(bf16[48,128,128]{2,1,0:T(8,128)(2,1)S(1)} %constant_dynamic-update-slice_fusion.5.mine_ref), channel_id=1, source_target_pairs={{0,8},{8,0},{1,9},{9,1},{2,10},{10,2},{3,11},{11,3},{4,12},{12,4},... | collective-permute-start | bytes 4718600 | tf_op jit(solution)/shard_map/ppermute | solution.py:35
  141.8 3.0 %collective-permute-done.13.other_ref = bf16[48,128,128]{2,1,0:T(8,128)(2,1)S(1)} collective-permute-done((bf16[48,128,128]{2,1,0:T(8,128)(2,1)S(1)}, bf16[48,128,128]{2,1,0:T(8,128)(2,1)S(1)}, u32[]{:S(2)}, u32[]{:S(2)}) %collective-permute-start.13) | collective-permute-done | bytes 1572896 | tf_op jit(solution)/shard_map/ppermute | solution.py:35
  144.8 1.6 pick.3
  146.4 0.6 broadcast_in_dim.17
  147.1 3.7 %all-to-all-start.4 = ((f32[12,16,128]{2,1,0:T(8,128)}), f32[12,16,128]{2,1,0:T(8,128)S(1)}, u32[]{:S(2)}, u32[]{:S(2)}) async-start(f32[12,16,128]{2,1,0:T(8,128)} %broadcast_in_dim.17), calls=%async_computation.4 | async-start | bytes 196608 | tf_op jit(solution)/shard_map/all_to_all | solution.py:31
  150.8 1.0 convert_reduce_fusion
  151.8 0.6 reshape.70.owner_ref
  152.4 3.8 %widen.1.wide_hbm = bf16[128,8192]{1,0:T(8,128)(2,1)} custom-call(s32[128]{0:T(128)} %reshape.70.owner_ref, bf16[8,33,16,128]{3,2,1,0:T(8,128)(2,1)} %bitcast.17.pack_ref.side_hbm), custom_call_target="tpu_custom_call" | custom-call | tf_op jit(solution)/shard_map/widen/pallas_call | solution.py:96
  156.2 4.7 %all-to-all-done.4 = f32[12,16,128]{2,1,0:T(8,128)S(1)} async-done(((f32[12,16,128]{2,1,0:T(8,128)}), f32[12,16,128]{2,1,0:T(8,128)S(1)}, u32[]{:S(2)}, u32[]{:S(2)}) %all-to-all-start.4) | async-done | bytes 98336 | tf_op jit(solution)/shard_map/all_to_all | solution.py:31
  160.9 10.3 %all_to_all.45 = f32[8,16,128]{2,1,0:T(8,128)S(1)} all-to-all(f32[8,16,128]{2,1,0:T(8,128)S(1)} %broadcast_in_dim.18), channel_id=1, replica_groups=mesh['x'=4,'z'=12,'core'=2,'items'=8] {'items'}, dimensions={0} | all-to-all | bytes 131072 | tf_op jit(solution)/shard_map/all_to_all | solution.py:31
  171.2 0.8 broadcast_in_dim.20
  172.0 6.8 %all-to-all-start.6 = ((f32[8,128,128]{2,1,0:T(8,128)}), f32[8,128,128]{2,1,0:T(8,128)S(1)}, u32[]{:S(2)}, u32[]{:S(2)}) async-start(f32[8,128,128]{2,1,0:T(8,128)} %broadcast_in_dim.20), calls=%async_computation.6 | async-start | bytes 1048576 | tf_op jit(solution)/shard_map/all_to_all | solution.py:31
  178.8 0.7 constant_dynamic-slice_fusion
  179.5 8.8 %all-to-all-done.6 = f32[8,128,128]{2,1,0:T(8,128)S(1)} async-done(((f32[8,128,128]{2,1,0:T(8,128)}), f32[8,128,128]{2,1,0:T(8,128)S(1)}, u32[]{:S(2)}, u32[]{:S(2)}) %all-to-all-start.6) | async-done | bytes 524320 | tf_op jit(solution)/shard_map/all_to_all | solution.py:31
  188.3 0.8 fusion.8
  189.1 13.1 %solve0.1 = (f32[8,64,128]{2,1,0:T(8,128)}, f32[64,512]{1,0:T(8,128)}, bf16[128,8192]{1,0:T(8,128)(2,1)}) custom-call(f32[64,512]{1,0:T(8,128)} %bitcast.66, f32[512,128]{1,0:T(8,128)} %bitcast.65, bf16[8192,256]{1,0:T(8,128)(2,1)} %all-gather.3.cloned.1.call-done.table_hbm, bf16[128,8192]{1,0:T(8,128)(2,1)} %widen.1.wide_hbm, ...), custom_call_target="tpu_custom_call" | custom-call | tf_op jit(solution)/shard_map/solve0/pallas_call | solution.py:249
  202.3 3.6 %all-to-all-start.7 = ((f32[8,64,128]{2,1,0:T(8,128)}), f32[8,64,128]{2,1,0:T(8,128)S(1)}, u32[]{:S(2)}, u32[]{:S(2)}) async-start(f32[8,64,128]{2,1,0:T(8,128)} %get-tuple-element.35), calls=%async_computation.7 | async-start | bytes 524288 | tf_op jit(solution)/shard_map/all_to_all | solution.py:352
  205.9 11.7 %solve1.1 = f32[8,64,128]{2,1,0:T(8,128)} custom-call(f32[64,512]{1,0:T(8,128)} %get-tuple-element.36.factors_hbm, f32[512,128]{1,0:T(8,128)} %bitcast.59, bf16[8192,256]{1,0:T(8,128)(2,1)} %all-gather.5.cloned.1.call-done.table_hbm, bf16[128,8192]{1,0:T(8,128)(2,1)} %widen.1.wide_hbm, bf16[128,8192]{1,0:T(8,128)(2,1)} %get-tuple-element.38.side_hbm), custom_call_target="tpu_custom_call" | custom-call | tf_op jit(solution)/shard_map/solve1/pallas_call | solution.py:249
  217.7 6.3 %all-to-all-start.8 = ((f32[8,64,128]{2,1,0:T(8,128)}), f32[8,64,128]{2,1,0:T(8,128)S(1)}, u32[]{:S(2)}, u32[]{:S(2)}) async-start(f32[8,64,128]{2,1,0:T(8,128)} %solve1.1), calls=%async_computation.8 | async-start | bytes 524288 | tf_op jit(solution)/shard_map/all_to_all | solution.py:352
  224.1 10.0 %all-to-all-done.8 = f32[8,64,128]{2,1,0:T(8,128)S(1)} async-done(((f32[8,64,128]{2,1,0:T(8,128)}), f32[8,64,128]{2,1,0:T(8,128)S(1)}, u32[]{:S(2)}, u32[]{:S(2)}) %all-to-all-start.8) | async-done | bytes 262176 | tf_op jit(solution)/shard_map/all_to_all | solution.py:352
  234.1 1.1 pad_maximum_fusion.1
  (48 shorter events, 0.6 us)
Async XLA Ops:
  6.5 22.9 %copy-start.1 = (bf16[1,1,16,128,128]{4,3,2,1,0:T(8,128)(2,1)S(1)}, bf16[1,1,16,128,128]{4,3,2,1,0:T(8,128)(2,1)}, u32[]{:S(2)}) copy-start(bf16[1,1,16,128,128]{4,3,2,1,0:T(8,128)(2,1)} %param.9) | copy-start | bytes 1572868
  8.8 20.7 %copy-start.6 = (s32[1,1,16]{2,1,0:T(1,128)S(1)}, s32[1,1,16]{2,1,0:T(1,128)}, u32[]{:S(2)}) copy-start(s32[1,1,16]{2,1,0:T(1,128)} %param.11) | copy-start | bytes 196
  8.8 20.8 %copy-start.2 = (bf16[1,1,16,128,128]{4,3,2,1,0:T(8,128)(2,1)S(1)}, bf16[1,1,16,128,128]{4,3,2,1,0:T(8,128)(2,1)}, u32[]{:S(2)}) copy-start(bf16[1,1,16,128,128]{4,3,2,1,0:T(8,128)(2,1)} %param.10) | copy-start | bytes 1572868
  8.8 34.5 %all-to-all-start = ((bf16[12,128,128]{2,1,0:T(8,128)(2,1)}), bf16[12,128,128]{2,1,0:T(8,128)(2,1)S(1)}, u32[]{:S(2)}, u32[]{:S(2)}) async-start(bf16[12,128,128]{2,1,0:T(8,128)(2,1)} %broadcast_in_dim.14), calls=%async_computation | async-start | bytes 786432 | tf_op jit(solution)/shard_map/all_to_all | solution.py:31
  25.9 5.1 %collective-permute-start = (f32[512,128]{1,0:T(8,128)S(1)}, f32[512,128]{1,0:T(8,128)S(1)}, u32[]{:S(2)}, u32[]{:S(2)}) collective-permute-start(f32[512,128]{1,0:T(8,128)S(1)} %slice_select_fusion), channel_id=1, source_target_pairs={{0,8},{8,0},{1,9},{9,1},{2,10},{10,2},{3,11},{11,3},{4,12},{12,4},... | collective-permute-start | bytes 786440 | tf_op jit(solution)/shard_map/ppermute | solution.py:35
  43.3 13.4 %collective-permute-start.1 = (bf16[12,128,128]{2,1,0:T(8,128)(2,1)S(1)}, bf16[12,128,128]{2,1,0:T(8,128)(2,1)S(1)}, u32[]{:S(2)}, u32[]{:S(2)}) collective-permute-start(bf16[12,128,128]{2,1,0:T(8,128)(2,1)S(1)} %all-to-all-done), channel_id=1, source_target_pairs={{0,192},{192,384},{384,576},{576,0},{1,193},{193,385},{385,577},{5... | collective-permute-start | bytes 1179656 | tf_op jit(solution)/shard_map/ppermute | solution.py:279
  46.5 12.3 %collective-permute-start.3 = (bf16[12,128,128]{2,1,0:T(8,128)(2,1)S(1)}, bf16[12,128,128]{2,1,0:T(8,128)(2,1)S(1)}, u32[]{:S(2)}, u32[]{:S(2)}) collective-permute-start(bf16[12,128,128]{2,1,0:T(8,128)(2,1)S(1)} %all-to-all-done), channel_id=1, source_target_pairs={{0,576},{192,0},{384,192},{576,384},{1,577},{193,1},{385,193},{577... | collective-permute-start | bytes 1179656 | tf_op jit(solution)/shard_map/ppermute | solution.py:279
  49.8 34.7 %all-to-all-start.1 = ((bf16[8,528,128]{2,1,0:T(8,128)(2,1)}), bf16[8,528,128]{2,1,0:T(8,128)(2,1)}, u32[]{:S(2)}, u32[]{:S(2)}) async-start(bf16[8,528,128]{2,1,0:T(8,128)(2,1)} %bitcast.11), calls=%async_computation.1 | async-start | bytes 2162688 | tf_op jit(solution)/shard_map/all_to_all | solution.py:317
  56.7 132.5 %all-gather.3.cloned.1.call-start = ((), (), s32[]{:S(2)}) async-start(), calls=%async_computation.9 | async-start | bytes 4718592 | tf_op jit(solution)/shard_map/all_gather | solution.py:320
  56.8 7.6 %collective-permute-start.2 = (bf16[6,128,128]{2,1,0:T(8,128)(2,1)S(1)}, bf16[6,128,128]{2,1,0:T(8,128)(2,1)S(1)}, u32[]{:S(2)}, u32[]{:S(2)}) collective-permute-start(bf16[6,128,128]{2,1,0:T(8,128)(2,1)S(1)} %slice.59), channel_id=1, source_target_pairs={{0,192},{192,384},{384,576},{576,0},{1,193},{193,385},{385,577},{5... | collective-permute-start | bytes 589832 | tf_op jit(solution)/shard_map/ppermute | solution.py:279
  58.7 13.2 %copy-start.5 = (s32[1,1,16]{2,1,0:T(1,128)S(1)}, s32[1,1,16]{2,1,0:T(1,128)}, u32[]{:S(2)}) copy-start(s32[1,1,16]{2,1,0:T(1,128)} %param.12) | copy-start | bytes 196
  58.8 7.2 %collective-permute-start.4 = (bf16[6,128,128]{2,1,0:T(8,128)(2,1)S(1)}, bf16[6,128,128]{2,1,0:T(8,128)(2,1)S(1)}, u32[]{:S(2)}, u32[]{:S(2)}) collective-permute-start(bf16[6,128,128]{2,1,0:T(8,128)(2,1)S(1)} %slice.60), channel_id=1, source_target_pairs={{0,576},{192,0},{384,192},{576,384},{1,577},{193,1},{385,193},{577... | collective-permute-start | bytes 589832 | tf_op jit(solution)/shard_map/ppermute | solution.py:279
  66.0 8.9 %collective-permute-start.5 = (bf16[48,128,128]{2,1,0:T(8,128)(2,1)S(1)}, bf16[48,128,128]{2,1,0:T(8,128)(2,1)S(1)}, u32[]{:S(2)}, u32[]{:S(2)}) collective-permute-start(bf16[48,128,128]{2,1,0:T(8,128)(2,1)S(1)} %constant_dynamic-update-slice_fusion.mine_ref), channel_id=1, source_target_pairs={{0,8},{8,0},{1,9},{9,1},{2,10},{10,2},{3,11},{11,3},{4,12},{12,4},... | collective-permute-start | bytes 4718600 | tf_op jit(solution)/shard_map/ppermute | solution.py:35
  72.0 12.6 %copy-start.4 = (bf16[128,128]{1,0:T(8,128)(2,1)S(1)}, bf16[128,128]{1,0:T(8,128)(2,1)}, u32[]{:S(2)}) copy-start(bf16[128,128]{1,0:T(8,128)(2,1)} %get-tuple-element.26) | copy-start | bytes 98308
  76.6 15.6 %copy-start = (f32[512,128]{1,0:T(8,128)S(1)}, f32[512,128]{1,0:T(8,128)}, u32[]{:S(2)}) copy-start(f32[512,128]{1,0:T(8,128)} %select_add_fusion) | copy-start | bytes 786436
  85.4 25.2 %all-to-all-start.2 = ((bf16[12,128,128]{2,1,0:T(8,128)(2,1)}), bf16[12,128,128]{2,1,0:T(8,128)(2,1)S(1)}, u32[]{:S(2)}, u32[]{:S(2)}) async-start(bf16[12,128,128]{2,1,0:T(8,128)(2,1)} %broadcast_in_dim.16), calls=%async_computation.2 | async-start | bytes 786432 | tf_op jit(solution)/shard_map/all_to_all | solution.py:31
  92.2 8.1 %collective-permute-start.8 = (f32[128,128]{1,0:T(8,128)S(1)}, f32[128,128]{1,0:T(8,128)S(1)}, u32[]{:S(2)}, u32[]{:S(2)}) collective-permute-start(f32[128,128]{1,0:T(8,128)S(1)} %get-tuple-element.42), channel_id=1, source_target_pairs={{0,576},{192,0},{384,192},{576,384},{1,577},{193,1},{385,193},{577... | collective-permute-start | bytes 196616 | tf_op jit(solution)/shard_map/ppermute | solution.py:279
  95.4 6.8 %collective-permute-start.7 = (f32[128,128]{1,0:T(8,128)S(1)}, f32[128,128]{1,0:T(8,128)S(1)}, u32[]{:S(2)}, u32[]{:S(2)}) collective-permute-start(f32[128,128]{1,0:T(8,128)S(1)} %get-tuple-element.43), channel_id=1, source_target_pairs={{0,384},{192,576},{384,0},{576,192},{1,385},{193,577},{385,1},{577... | collective-permute-start | bytes 196616 | tf_op jit(solution)/shard_map/ppermute | solution.py:279
  97.8 6.7 %collective-permute-start.6 = (f32[128,128]{1,0:T(8,128)S(1)}, f32[128,128]{1,0:T(8,128)S(1)}, u32[]{:S(2)}, u32[]{:S(2)}) collective-permute-start(f32[128,128]{1,0:T(8,128)S(1)} %get-tuple-element.41), channel_id=1, source_target_pairs={{0,192},{192,384},{384,576},{576,0},{1,193},{193,385},{385,577},{5... | collective-permute-start | bytes 196616 | tf_op jit(solution)/shard_map/ppermute | solution.py:279
  110.7 11.7 %collective-permute-start.9 = (bf16[12,128,128]{2,1,0:T(8,128)(2,1)S(1)}, bf16[12,128,128]{2,1,0:T(8,128)(2,1)S(1)}, u32[]{:S(2)}, u32[]{:S(2)}) collective-permute-start(bf16[12,128,128]{2,1,0:T(8,128)(2,1)S(1)} %all-to-all-done.2), channel_id=1, source_target_pairs={{0,192},{192,384},{384,576},{576,0},{1,193},{193,385},{385,577},{5... | collective-permute-start | bytes 1179656 | tf_op jit(solution)/shard_map/ppermute | solution.py:279
  112.6 15.8 %collective-permute-start.11 = (bf16[12,128,128]{2,1,0:T(8,128)(2,1)S(1)}, bf16[12,128,128]{2,1,0:T(8,128)(2,1)S(1)}, u32[]{:S(2)}, u32[]{:S(2)}) collective-permute-start(bf16[12,128,128]{2,1,0:T(8,128)(2,1)S(1)} %all-to-all-done.2), channel_id=1, source_target_pairs={{0,576},{192,0},{384,192},{576,384},{1,577},{193,1},{385,193},{577... | collective-permute-start | bytes 1179656 | tf_op jit(solution)/shard_map/ppermute | solution.py:279
  117.2 11.2 %all-to-all-start.3 = ((f32[8,16,128]{2,1,0:T(8,128)}), f32[8,16,128]{2,1,0:T(8,128)S(1)}, u32[]{:S(2)}, u32[]{:S(2)}) async-start(f32[8,16,128]{2,1,0:T(8,128)} %bitcast.16), calls=%async_computation.3 | async-start | bytes 131072 | tf_op jit(solution)/shard_map/all_to_all | solution.py:331
  120.5 85.4 %all-gather.5.cloned.1.call-start = ((), (), s32[]{:S(2)}) async-start(), calls=%async_computation.10 | async-start | bytes 4718592 | tf_op jit(solution)/shard_map/all_gather | solution.py:334
  122.4 8.1 %collective-permute-start.10 = (bf16[6,128,128]{2,1,0:T(8,128)(2,1)S(1)}, bf16[6,128,128]{2,1,0:T(8,128)(2,1)S(1)}, u32[]{:S(2)}, u32[]{:S(2)}) collective-permute-start(bf16[6,128,128]{2,1,0:T(8,128)(2,1)S(1)} %slice.61), channel_id=1, source_target_pairs={{0,192},{192,384},{384,576},{576,0},{1,193},{193,385},{385,577},{5... | collective-permute-start | bytes 589832 | tf_op jit(solution)/shard_map/ppermute | solution.py:279
  128.4 6.8 %collective-permute-start.12 = (bf16[6,128,128]{2,1,0:T(8,128)(2,1)S(1)}, bf16[6,128,128]{2,1,0:T(8,128)(2,1)S(1)}, u32[]{:S(2)}, u32[]{:S(2)}) collective-permute-start(bf16[6,128,128]{2,1,0:T(8,128)(2,1)S(1)} %slice.62), channel_id=1, source_target_pairs={{0,576},{192,0},{384,192},{576,384},{1,577},{193,1},{385,193},{577... | collective-permute-start | bytes 589832 | tf_op jit(solution)/shard_map/ppermute | solution.py:279
  135.3 9.5 %collective-permute-start.13 = (bf16[48,128,128]{2,1,0:T(8,128)(2,1)S(1)}, bf16[48,128,128]{2,1,0:T(8,128)(2,1)S(1)}, u32[]{:S(2)}, u32[]{:S(2)}) collective-permute-start(bf16[48,128,128]{2,1,0:T(8,128)(2,1)S(1)} %constant_dynamic-update-slice_fusion.5.mine_ref), channel_id=1, source_target_pairs={{0,8},{8,0},{1,9},{9,1},{2,10},{10,2},{3,11},{11,3},{4,12},{12,4},... | collective-permute-start | bytes 4718600 | tf_op jit(solution)/shard_map/ppermute | solution.py:35
  147.1 13.8 %all-to-all-start.4 = ((f32[12,16,128]{2,1,0:T(8,128)}), f32[12,16,128]{2,1,0:T(8,128)S(1)}, u32[]{:S(2)}, u32[]{:S(2)}) async-start(f32[12,16,128]{2,1,0:T(8,128)} %broadcast_in_dim.17), calls=%async_computation.4 | async-start | bytes 196608 | tf_op jit(solution)/shard_map/all_to_all | solution.py:31
  156.2 22.6 %copy-start.3 = (f32[512,512]{1,0:T(8,128)S(1)}, f32[512,512]{1,0:T(8,128)}, u32[]{:S(2)}) copy-start(f32[512,512]{1,0:T(8,128)} %param.7) | copy-start | bytes 3145732
  172.0 16.3 %all-to-all-start.6 = ((f32[8,128,128]{2,1,0:T(8,128)}), f32[8,128,128]{2,1,0:T(8,128)S(1)}, u32[]{:S(2)}, u32[]{:S(2)}) async-start(f32[8,128,128]{2,1,0:T(8,128)} %broadcast_in_dim.20), calls=%async_computation.6 | async-start | bytes 1048576 | tf_op jit(solution)/shard_map/all_to_all | solution.py:31
  202.3 15.4 %all-to-all-start.7 = ((f32[8,64,128]{2,1,0:T(8,128)}), f32[8,64,128]{2,1,0:T(8,128)S(1)}, u32[]{:S(2)}, u32[]{:S(2)}) async-start(f32[8,64,128]{2,1,0:T(8,128)} %get-tuple-element.35), calls=%async_computation.7 | async-start | bytes 524288 | tf_op jit(solution)/shard_map/all_to_all | solution.py:352
  217.7 16.4 %all-to-all-start.8 = ((f32[8,64,128]{2,1,0:T(8,128)}), f32[8,64,128]{2,1,0:T(8,128)S(1)}, u32[]{:S(2)}, u32[]{:S(2)}) async-start(f32[8,64,128]{2,1,0:T(8,128)} %solve1.1), calls=%async_computation.8 | async-start | bytes 524288 | tf_op jit(solution)/shard_map/all_to_all | solution.py:352
Sparse Core Ops, SparseCore 0:
  84.7 53.1 all-gather.2
  146.6 54.0 all-gather.4

commit v3 on v2

--- a/solution.py
+++ b/solution.py
@@ -28,6 +28,23 @@
 def spread(value, axis):
     n = lax.axis_size(axis)
     copies = jnp.broadcast_to(value[None], (n,) + value.shape)
+    return lax.all_to_all(copies, axis, 0, 0)
+
+
+def copy_kernel(items_ref, out_ref):
+    columns = items_ref[:, :BLK]
+    for copy in range(out_ref.shape[0]):
+        out_ref[copy] = columns
+
+
+def spread_first(items, axis):
+    copies = pl.pallas_call(
+        copy_kernel,
+        out_shape=jax.ShapeDtypeStruct((lax.axis_size(axis), items.shape[0], BLK), items.dtype),
+        in_specs=[pl.BlockSpec(memory_space=pltpu.VMEM)],
+        out_specs=pl.BlockSpec(memory_space=pltpu.VMEM),
+        name="copies",
+    )(items)
     return lax.all_to_all(copies, axis, 0, 0)
 
 
@@ -311,7 +328,7 @@
         opposite = [along_x(behind[:middle], 1), along_x(ahead[middle:], -1)]
         return jnp.concatenate([blocks, behind, *opposite, ahead], axis=0)
 
-    line0 = spread(own_items[:, :BLK], "z")
+    line0 = spread_first(own_items, "z")
     line0, parts, pack = lax.optimization_barrier((line0, parts, pack))
     mine0 = round_x(line0)
     pack = lax.all_to_all(pack, "items", 0, 0)
@@ -354,9 +371,8 @@
 
     news0, factors, errors = solve(0, implicit, n_items, factors, gram0, table0, wide, pack)
     (news1,) = solve(1, implicit, n_items, factors, gram1, table1, wide, errors)
-    return jnp.concatenate(
-        [all_users(news0), all_users(news1), user_factors[:, width:]], axis=1
-    )
+    result = jnp.concatenate([all_users(news0), user_factors[:, BLK:]], axis=1)
+    return lax.dynamic_update_slice(result, all_users(news1), (0, BLK))
 
 
 def solution(mesh):

time: 244 us -> 244 us (level)
    all_to_all x4 -> x3, starting transfers between devices: 33 us -> 17.2 us  [spread(): return lax.all_to_all(copies, axis, 0, 0)]
    all_to_all x0 -> x1, starting transfers between devices: none -> 15.8 us  [spread_first(): return lax.all_to_all(copies, axis, 0, 0)]
    all_to_all x0 -> x1, waiting for transfers between devices: none -> 11.7 us  [spread_first(): return lax.all_to_all(copies, axis, 0, 0)]
    all_to_all x4 -> x3, waiting for transfers between devices: 30.7 us -> 19.1 us  [spread(): return lax.all_to_all(copies, axis, 0, 0)]
  transfers between devices with their start and end apart: 24 -> 24, of which waited for: 15 -> 15; matrix products, arithmetic and copies ran while one was open for 4% -> 5% of each run, Pallas kernels for 13% -> 13%
where the time goes in v3:
time: 244 us; the launch traced here: 242 us
  starting transfers between devices  100 us (41%)
  waiting for transfers between devices  70.9 us (29%)
  Pallas kernels  33.6 us (14%)
  between operations  14.6 us (6%)
  blocking collectives  10.3 us (4%)
  local copies, waits for them, and re-layouts  7.66 us (3%)
  other arithmetic  3.82 us (2%)
    ppermute x11, starting transfers between devices, along_x(): lax.ppermute(value, 'x', [(i, (i + shift) % n_x) for i in range(n_x)])  31.5 us
    pallas_call x2, Pallas kernels, solve(): pl.pallas_call(functools.partial(solve_kernel, block * BLK, implicit, las...  24.8 us
    all_to_all x3, waiting for transfers between devices, spread(): return lax.all_to_all(copies, axis, 0, 0)  19.1 us
    all_to_all x3, starting transfers between devices, spread(): return lax.all_to_all(copies, axis, 0, 0)  17.2 us
    all_to_all x1, starting transfers between devices, spread_first(): return lax.all_to_all(copies, axis, 0, 0)  15.8 us
    ppermute x3, starting transfers between devices, swap_cores(): return lax.ppermute(value, 'core', [(0, 1), (1, 0)])  15.3 us
    ppermute x11, waiting for transfers between devices, along_x(): lax.ppermute(value, 'x', [(i, (i + shift) % n_x) for i in range(n_x)])  13.2 us
    all_to_all x1, waiting for transfers between devices, spread_first(): return lax.all_to_all(copies, axis, 0, 0)  11.7 us
  transfers between devices with their start and end apart: 24, of which 15 were waited for; matrix products, arithmetic and copies ran while one was open for 5% of the time, Pallas kernels for 13%

profile of v3, /device:TPU:1, one launch (start us, length us, event | category | flops | bytes accessed | tf_op | source)
XLA Modules:
  0.0 241.9 jit_solution(1512450311412944248)
XLA Ops:
  6.5 1.8 copies.1
  8.3 15.8 %all-to-all-start = ((bf16[12,128,128]{2,1,0:T(8,128)(2,1)}), bf16[12,128,128]{2,1,0:T(8,128)(2,1)S(1)}, u32[]{:S(2)}, u32[]{:S(2)}) async-start(bf16[12,128,128]{2,1,0:T(8,128)(2,1)} %copies.1), calls=%async_computation | async-start | bytes 786432 | tf_op jit(solution)/shard_map/all_to_all | solution.py:48
  24.2 1.2 fusion
  25.4 2.9 %collective-permute-start = (f32[512,128]{1,0:T(8,128)S(1)}, f32[512,128]{1,0:T(8,128)S(1)}, u32[]{:S(2)}, u32[]{:S(2)}) collective-permute-start(f32[512,128]{1,0:T(8,128)S(1)} %slice_select_fusion), channel_id=1, source_target_pairs={{0,8},{8,0},{1,9},{9,1},{2,10},{10,2},{3,11},{11,3},{4,12},{12,4},... | collective-permute-start | bytes 786440 | tf_op jit(solution)/shard_map/ppermute | solution.py:52
  28.9 0.1 multiply_bitcast_fusion
  29.0 0.1 broadcast_in_dim.12
  29.1 0.1 pad_maximum_fusion
  29.3 1.2 copy.17
  30.4 0.8 select_add_fusion
  31.2 11.7 %all-to-all-done = bf16[12,128,128]{2,1,0:T(8,128)(2,1)S(1)} async-done(((bf16[12,128,128]{2,1,0:T(8,128)(2,1)}), bf16[12,128,128]{2,1,0:T(8,128)(2,1)S(1)}, u32[]{:S(2)}, u32[]{:S(2)}) %all-to-all-start) | async-done | bytes 393248 | tf_op jit(solution)/shard_map/all_to_all | solution.py:48
  42.9 3.1 %collective-permute-start.1 = (bf16[12,128,128]{2,1,0:T(8,128)(2,1)S(1)}, bf16[12,128,128]{2,1,0:T(8,128)(2,1)S(1)}, u32[]{:S(2)}, u32[]{:S(2)}) collective-permute-start(bf16[12,128,128]{2,1,0:T(8,128)(2,1)S(1)} %all-to-all-done), channel_id=1, source_target_pairs={{0,192},{192,384},{384,576},{576,0},{1,193},{193,385},{385,577},{5... | collective-permute-start | bytes 1179656 | tf_op jit(solution)/shard_map/ppermute | solution.py:296
  46.0 3.4 %collective-permute-start.3 = (bf16[12,128,128]{2,1,0:T(8,128)(2,1)S(1)}, bf16[12,128,128]{2,1,0:T(8,128)(2,1)S(1)}, u32[]{:S(2)}, u32[]{:S(2)}) collective-permute-start(bf16[12,128,128]{2,1,0:T(8,128)(2,1)S(1)} %all-to-all-done), channel_id=1, source_target_pairs={{0,576},{192,0},{384,192},{576,384},{1,577},{193,1},{385,193},{577... | collective-permute-start | bytes 1179656 | tf_op jit(solution)/shard_map/ppermute | solution.py:296
  49.4 6.8 %all-to-all-start.1 = ((bf16[8,528,128]{2,1,0:T(8,128)(2,1)}), bf16[8,528,128]{2,1,0:T(8,128)(2,1)}, u32[]{:S(2)}, u32[]{:S(2)}) async-start(bf16[8,528,128]{2,1,0:T(8,128)(2,1)} %bitcast.11), calls=%async_computation.1 | async-start | bytes 2162688 | tf_op jit(solution)/shard_map/all_to_all | solution.py:334
  56.3 1.9 collective-permute-start.2
  58.3 4.6 %collective-permute-start.4 = (bf16[6,128,128]{2,1,0:T(8,128)(2,1)S(1)}, bf16[6,128,128]{2,1,0:T(8,128)(2,1)S(1)}, u32[]{:S(2)}, u32[]{:S(2)}) collective-permute-start(bf16[6,128,128]{2,1,0:T(8,128)(2,1)S(1)} %slice.55), channel_id=1, source_target_pairs={{0,576},{192,0},{384,192},{576,384},{1,577},{193,1},{385,193},{577... | collective-permute-start | bytes 589832 | tf_op jit(solution)/shard_map/ppermute | solution.py:296
  62.9 1.0 collective-permute-done.2
  63.9 1.5 collective-permute-done.4
  65.5 5.9 %collective-permute-start.5 = (bf16[48,128,128]{2,1,0:T(8,128)(2,1)S(1)}, bf16[48,128,128]{2,1,0:T(8,128)(2,1)S(1)}, u32[]{:S(2)}, u32[]{:S(2)}) collective-permute-start(bf16[48,128,128]{2,1,0:T(8,128)(2,1)S(1)} %constant_dynamic-update-slice_fusion.mine_ref), channel_id=1, source_target_pairs={{0,8},{8,0},{1,9},{9,1},{2,10},{10,2},{3,11},{11,3},{4,12},{12,4},... | collective-permute-start | bytes 4718600 | tf_op jit(solution)/shard_map/ppermute | solution.py:52
  71.5 3.0 %collective-permute-done.5.other_ref = bf16[48,128,128]{2,1,0:T(8,128)(2,1)S(1)} collective-permute-done((bf16[48,128,128]{2,1,0:T(8,128)(2,1)S(1)}, bf16[48,128,128]{2,1,0:T(8,128)(2,1)S(1)}, u32[]{:S(2)}, u32[]{:S(2)}) %collective-permute-start.5) | collective-permute-done | bytes 1572896 | tf_op jit(solution)/shard_map/ppermute | solution.py:52
  74.5 1.6 pick.2
  76.1 8.0 %all-to-all-done.1 = bf16[8,528,128]{2,1,0:T(8,128)(2,1)} async-done(((bf16[8,528,128]{2,1,0:T(8,128)(2,1)}), bf16[8,528,128]{2,1,0:T(8,128)(2,1)}, u32[]{:S(2)}, u32[]{:S(2)}) %all-to-all-start.1) | async-done | bytes 1081376 | tf_op jit(solution)/shard_map/all_to_all | solution.py:334
  84.1 0.8 slice.50
  84.9 0.8 broadcast_in_dim.13
  85.7 6.6 %all-to-all-start.2 = ((bf16[12,128,128]{2,1,0:T(8,128)(2,1)}), bf16[12,128,128]{2,1,0:T(8,128)(2,1)S(1)}, u32[]{:S(2)}, u32[]{:S(2)}) async-start(bf16[12,128,128]{2,1,0:T(8,128)(2,1)} %broadcast_in_dim.13), calls=%async_computation.2 | async-start | bytes 786432 | tf_op jit(solution)/shard_map/all_to_all | solution.py:31
  92.4 3.2 %collective-permute-start.8 = (f32[128,128]{1,0:T(8,128)S(1)}, f32[128,128]{1,0:T(8,128)S(1)}, u32[]{:S(2)}, u32[]{:S(2)}) collective-permute-start(f32[128,128]{1,0:T(8,128)S(1)} %get-tuple-element.42), channel_id=1, source_target_pairs={{0,576},{192,0},{384,192},{576,384},{1,577},{193,1},{385,193},{577... | collective-permute-start | bytes 196616 | tf_op jit(solution)/shard_map/ppermute | solution.py:296
  95.6 2.4 %collective-permute-start.7 = (f32[128,128]{1,0:T(8,128)S(1)}, f32[128,128]{1,0:T(8,128)S(1)}, u32[]{:S(2)}, u32[]{:S(2)}) collective-permute-start(f32[128,128]{1,0:T(8,128)S(1)} %get-tuple-element.43), channel_id=1, source_target_pairs={{0,384},{192,576},{384,0},{576,192},{1,385},{193,577},{385,1},{577... | collective-permute-start | bytes 196616 | tf_op jit(solution)/shard_map/ppermute | solution.py:296
  98.1 2.5 %collective-permute-start.6 = (f32[128,128]{1,0:T(8,128)S(1)}, f32[128,128]{1,0:T(8,128)S(1)}, u32[]{:S(2)}, u32[]{:S(2)}) collective-permute-start(f32[128,128]{1,0:T(8,128)S(1)} %get-tuple-element.41), channel_id=1, source_target_pairs={{0,192},{192,384},{384,576},{576,0},{1,193},{193,385},{385,577},{5... | collective-permute-start | bytes 196616 | tf_op jit(solution)/shard_map/ppermute | solution.py:296
  100.6 1.8 collective-permute-done.7
  102.4 2.3 collective-permute-done.6
  104.8 0.6 fusion.3
  105.4 5.5 %all-to-all-done.2 = bf16[12,128,128]{2,1,0:T(8,128)(2,1)S(1)} async-done(((bf16[12,128,128]{2,1,0:T(8,128)(2,1)}), bf16[12,128,128]{2,1,0:T(8,128)(2,1)S(1)}, u32[]{:S(2)}, u32[]{:S(2)}) %all-to-all-start.2) | async-done | bytes 393248 | tf_op jit(solution)/shard_map/all_to_all | solution.py:31
  110.9 1.9 collective-permute-start.9
  112.8 4.6 %collective-permute-start.11 = (bf16[12,128,128]{2,1,0:T(8,128)(2,1)S(1)}, bf16[12,128,128]{2,1,0:T(8,128)(2,1)S(1)}, u32[]{:S(2)}, u32[]{:S(2)}) collective-permute-start(bf16[12,128,128]{2,1,0:T(8,128)(2,1)S(1)} %all-to-all-done.2), channel_id=1, source_target_pairs={{0,576},{192,0},{384,192},{576,384},{1,577},{193,1},{385,193},{577... | collective-permute-start | bytes 1179656 | tf_op jit(solution)/shard_map/ppermute | solution.py:296
  117.4 3.4 %all-to-all-start.3 = ((f32[8,16,128]{2,1,0:T(8,128)}), f32[8,16,128]{2,1,0:T(8,128)S(1)}, u32[]{:S(2)}, u32[]{:S(2)}) async-start(f32[8,16,128]{2,1,0:T(8,128)} %bitcast.16), calls=%async_computation.3 | async-start | bytes 131072 | tf_op jit(solution)/shard_map/all_to_all | solution.py:348
  120.8 1.8 collective-permute-done.9
  122.6 1.9 collective-permute-start.10
  124.6 4.0 %all-to-all-done.3 = f32[8,16,128]{2,1,0:T(8,128)S(1)} async-done(((f32[8,16,128]{2,1,0:T(8,128)}), f32[8,16,128]{2,1,0:T(8,128)S(1)}, u32[]{:S(2)}, u32[]{:S(2)}) %all-to-all-start.3) | async-done | bytes 65568 | tf_op jit(solution)/shard_map/all_to_all | solution.py:348
  128.7 2.0 collective-permute-start.12
  130.6 0.1 constant_dynamic-update-slice_fusion.8
  130.7 4.7 %collective-permute-done.12 = bf16[6,128,128]{2,1,0:T(8,128)(2,1)S(1)} collective-permute-done((bf16[6,128,128]{2,1,0:T(8,128)(2,1)S(1)}, bf16[6,128,128]{2,1,0:T(8,128)(2,1)S(1)}, u32[]{:S(2)}, u32[]{:S(2)}) %collective-permute-start.12) | collective-permute-done | bytes 196640 | tf_op jit(solution)/shard_map/ppermute | solution.py:296
  135.5 0.1 constant_dynamic-update-slice_fusion.5.mine_ref
  135.6 6.5 %collective-permute-start.13 = (bf16[48,128,128]{2,1,0:T(8,128)(2,1)S(1)}, bf16[48,128,128]{2,1,0:T(8,128)(2,1)S(1)}, u32[]{:S(2)}, u32[]{:S(2)}) collective-permute-start(bf16[48,128,128]{2,1,0:T(8,128)(2,1)S(1)} %constant_dynamic-update-slice_fusion.5.mine_ref), channel_id=1, source_target_pairs={{0,8},{8,0},{1,9},{9,1},{2,10},{10,2},{3,11},{11,3},{4,12},{12,4},... | collective-permute-start | bytes 4718600 | tf_op jit(solution)/shard_map/ppermute | solution.py:52
  142.1 3.0 %collective-permute-done.13.other_ref = bf16[48,128,128]{2,1,0:T(8,128)(2,1)S(1)} collective-permute-done((bf16[48,128,128]{2,1,0:T(8,128)(2,1)S(1)}, bf16[48,128,128]{2,1,0:T(8,128)(2,1)S(1)}, u32[]{:S(2)}, u32[]{:S(2)}) %collective-permute-start.13) | collective-permute-done | bytes 1572896 | tf_op jit(solution)/shard_map/ppermute | solution.py:52
  145.1 1.6 pick.3
  146.7 0.6 broadcast_in_dim.14
  147.4 3.7 %all-to-all-start.4 = ((f32[12,16,128]{2,1,0:T(8,128)}), f32[12,16,128]{2,1,0:T(8,128)S(1)}, u32[]{:S(2)}, u32[]{:S(2)}) async-start(f32[12,16,128]{2,1,0:T(8,128)} %broadcast_in_dim.14), calls=%async_computation.4 | async-start | bytes 196608 | tf_op jit(solution)/shard_map/all_to_all | solution.py:31
  151.1 1.0 convert_reduce_fusion
  152.1 0.6 reshape.69.owner_ref
  152.6 3.8 %widen.1.wide_hbm = bf16[128,8192]{1,0:T(8,128)(2,1)} custom-call(s32[128]{0:T(128)} %reshape.69.owner_ref, bf16[8,33,16,128]{3,2,1,0:T(8,128)(2,1)} %bitcast.17.pack_ref.side_hbm), custom_call_target="tpu_custom_call" | custom-call | tf_op jit(solution)/shard_map/widen/pallas_call | solution.py:113
  156.4 4.7 %all-to-all-done.4 = f32[12,16,128]{2,1,0:T(8,128)S(1)} async-done(((f32[12,16,128]{2,1,0:T(8,128)}), f32[12,16,128]{2,1,0:T(8,128)S(1)}, u32[]{:S(2)}, u32[]{:S(2)}) %all-to-all-start.4) | async-done | bytes 98336 | tf_op jit(solution)/shard_map/all_to_all | solution.py:31
  161.2 10.3 %all_to_all.45 = f32[8,16,128]{2,1,0:T(8,128)S(1)} all-to-all(f32[8,16,128]{2,1,0:T(8,128)S(1)} %broadcast_in_dim.15), channel_id=1, replica_groups=mesh['x'=4,'z'=12,'core'=2,'items'=8] {'items'}, dimensions={0} | all-to-all | bytes 131072 | tf_op jit(solution)/shard_map/all_to_all | solution.py:31
  171.5 0.8 broadcast_in_dim.17
  172.3 6.8 %all-to-all-start.6 = ((f32[8,128,128]{2,1,0:T(8,128)}), f32[8,128,128]{2,1,0:T(8,128)S(1)}, u32[]{:S(2)}, u32[]{:S(2)}) async-start(f32[8,128,128]{2,1,0:T(8,128)} %broadcast_in_dim.17), calls=%async_computation.6 | async-start | bytes 1048576 | tf_op jit(solution)/shard_map/all_to_all | solution.py:31
  179.1 0.7 constant_dynamic-slice_fusion
  179.7 8.8 %all-to-all-done.6 = f32[8,128,128]{2,1,0:T(8,128)S(1)} async-done(((f32[8,128,128]{2,1,0:T(8,128)}), f32[8,128,128]{2,1,0:T(8,128)S(1)}, u32[]{:S(2)}, u32[]{:S(2)}) %all-to-all-start.6) | async-done | bytes 524320 | tf_op jit(solution)/shard_map/all_to_all | solution.py:31
  188.6 0.8 fusion.8
  189.4 13.1 %solve0.1 = (f32[8,64,128]{2,1,0:T(8,128)}, f32[64,512]{1,0:T(8,128)}, bf16[128,8192]{1,0:T(8,128)(2,1)}) custom-call(f32[64,512]{1,0:T(8,128)} %bitcast.70, f32[512,128]{1,0:T(8,128)} %bitcast.65, bf16[8192,256]{1,0:T(8,128)(2,1)} %all-gather.3.cloned.1.call-done.table_hbm, bf16[128,8192]{1,0:T(8,128)(2,1)} %widen.1.wide_hbm, ...), custom_call_target="tpu_custom_call" | custom-call | tf_op jit(solution)/shard_map/solve0/pallas_call | solution.py:266
  202.5 3.6 %all-to-all-start.7 = ((f32[8,64,128]{2,1,0:T(8,128)}), f32[8,64,128]{2,1,0:T(8,128)S(1)}, u32[]{:S(2)}, u32[]{:S(2)}) async-start(f32[8,64,128]{2,1,0:T(8,128)} %get-tuple-element.35), calls=%async_computation.7 | async-start | bytes 524288 | tf_op jit(solution)/shard_map/all_to_all | solution.py:369
  206.2 11.7 %solve1.1 = f32[8,64,128]{2,1,0:T(8,128)} custom-call(f32[64,512]{1,0:T(8,128)} %get-tuple-element.36.factors_hbm, f32[512,128]{1,0:T(8,128)} %bitcast.59, bf16[8192,256]{1,0:T(8,128)(2,1)} %all-gather.5.cloned.1.call-done.table_hbm, bf16[128,8192]{1,0:T(8,128)(2,1)} %widen.1.wide_hbm, bf16[128,8192]{1,0:T(8,128)(2,1)} %get-tuple-element.38.side_hbm), custom_call_target="tpu_custom_call" | custom-call | tf_op jit(solution)/shard_map/solve1/pallas_call | solution.py:266
  217.9 6.3 %all-to-all-start.8 = ((f32[8,64,128]{2,1,0:T(8,128)}), f32[8,64,128]{2,1,0:T(8,128)S(1)}, u32[]{:S(2)}, u32[]{:S(2)}) async-start(f32[8,64,128]{2,1,0:T(8,128)} %solve1.1), calls=%async_computation.8 | async-start | bytes 524288 | tf_op jit(solution)/shard_map/all_to_all | solution.py:369
  224.3 0.1 slice.48
  224.4 1.1 pad_maximum_fusion.1
  225.5 8.9 %all-to-all-done.8 = f32[8,64,128]{2,1,0:T(8,128)S(1)} async-done(((f32[8,64,128]{2,1,0:T(8,128)}), f32[8,64,128]{2,1,0:T(8,128)S(1)}, u32[]{:S(2)}, u32[]{:S(2)}) %all-to-all-start.8) | async-done | bytes 262176 | tf_op jit(solution)/shard_map/all_to_all | solution.py:369
  234.4 0.7 constant_dynamic-update-slice_fusion.10
  (47 shorter events, 0.7 us)
Async XLA Ops:
  6.5 22.4 %copy-start.2 = (bf16[1,1,16,128,128]{4,3,2,1,0:T(8,128)(2,1)S(1)}, bf16[1,1,16,128,128]{4,3,2,1,0:T(8,128)(2,1)}, u32[]{:S(2)}) copy-start(bf16[1,1,16,128,128]{4,3,2,1,0:T(8,128)(2,1)} %param.9) | copy-start | bytes 1572868
  8.3 20.7 %copy-start.5 = (s32[1,1,16]{2,1,0:T(1,128)S(1)}, s32[1,1,16]{2,1,0:T(1,128)}, u32[]{:S(2)}) copy-start(s32[1,1,16]{2,1,0:T(1,128)} %param.11) | copy-start | bytes 196
  8.3 20.8 %copy-start.3 = (bf16[1,1,16,128,128]{4,3,2,1,0:T(8,128)(2,1)S(1)}, bf16[1,1,16,128,128]{4,3,2,1,0:T(8,128)(2,1)}, u32[]{:S(2)}) copy-start(bf16[1,1,16,128,128]{4,3,2,1,0:T(8,128)(2,1)} %param.10) | copy-start | bytes 1572868
  8.3 34.5 %all-to-all-start = ((bf16[12,128,128]{2,1,0:T(8,128)(2,1)}), bf16[12,128,128]{2,1,0:T(8,128)(2,1)S(1)}, u32[]{:S(2)}, u32[]{:S(2)}) async-start(bf16[12,128,128]{2,1,0:T(8,128)(2,1)} %copies.1), calls=%async_computation | async-start | bytes 786432 | tf_op jit(solution)/shard_map/all_to_all | solution.py:48
  25.4 5.1 %collective-permute-start = (f32[512,128]{1,0:T(8,128)S(1)}, f32[512,128]{1,0:T(8,128)S(1)}, u32[]{:S(2)}, u32[]{:S(2)}) collective-permute-start(f32[512,128]{1,0:T(8,128)S(1)} %slice_select_fusion), channel_id=1, source_target_pairs={{0,8},{8,0},{1,9},{9,1},{2,10},{10,2},{3,11},{11,3},{4,12},{12,4},... | collective-permute-start | bytes 786440 | tf_op jit(solution)/shard_map/ppermute | solution.py:52
  42.9 13.4 %collective-permute-start.1 = (bf16[12,128,128]{2,1,0:T(8,128)(2,1)S(1)}, bf16[12,128,128]{2,1,0:T(8,128)(2,1)S(1)}, u32[]{:S(2)}, u32[]{:S(2)}) collective-permute-start(bf16[12,128,128]{2,1,0:T(8,128)(2,1)S(1)} %all-to-all-done), channel_id=1, source_target_pairs={{0,192},{192,384},{384,576},{576,0},{1,193},{193,385},{385,577},{5... | collective-permute-start | bytes 1179656 | tf_op jit(solution)/shard_map/ppermute | solution.py:296
  46.0 12.3 %collective-permute-start.3 = (bf16[12,128,128]{2,1,0:T(8,128)(2,1)S(1)}, bf16[12,128,128]{2,1,0:T(8,128)(2,1)S(1)}, u32[]{:S(2)}, u32[]{:S(2)}) collective-permute-start(bf16[12,128,128]{2,1,0:T(8,128)(2,1)S(1)} %all-to-all-done), channel_id=1, source_target_pairs={{0,576},{192,0},{384,192},{576,384},{1,577},{193,1},{385,193},{577... | collective-permute-start | bytes 1179656 | tf_op jit(solution)/shard_map/ppermute | solution.py:296
  49.4 34.7 %all-to-all-start.1 = ((bf16[8,528,128]{2,1,0:T(8,128)(2,1)}), bf16[8,528,128]{2,1,0:T(8,128)(2,1)}, u32[]{:S(2)}, u32[]{:S(2)}) async-start(bf16[8,528,128]{2,1,0:T(8,128)(2,1)} %bitcast.11), calls=%async_computation.1 | async-start | bytes 2162688 | tf_op jit(solution)/shard_map/all_to_all | solution.py:334
  56.2 133.2 %all-gather.3.cloned.1.call-start = ((), (), s32[]{:S(2)}) async-start(), calls=%async_computation.9 | async-start | bytes 4718592 | tf_op jit(solution)/shard_map/all_gather | solution.py:337
  56.3 7.6 %collective-permute-start.2 = (bf16[6,128,128]{2,1,0:T(8,128)(2,1)S(1)}, bf16[6,128,128]{2,1,0:T(8,128)(2,1)S(1)}, u32[]{:S(2)}, u32[]{:S(2)}) collective-permute-start(bf16[6,128,128]{2,1,0:T(8,128)(2,1)S(1)} %slice.54), channel_id=1, source_target_pairs={{0,192},{192,384},{384,576},{576,0},{1,193},{193,385},{385,577},{5... | collective-permute-start | bytes 589832 | tf_op jit(solution)/shard_map/ppermute | solution.py:296
  58.2 13.2 %copy-start.4 = (s32[1,1,16]{2,1,0:T(1,128)S(1)}, s32[1,1,16]{2,1,0:T(1,128)}, u32[]{:S(2)}) copy-start(s32[1,1,16]{2,1,0:T(1,128)} %param.12) | copy-start | bytes 196
  58.3 7.2 %collective-permute-start.4 = (bf16[6,128,128]{2,1,0:T(8,128)(2,1)S(1)}, bf16[6,128,128]{2,1,0:T(8,128)(2,1)S(1)}, u32[]{:S(2)}, u32[]{:S(2)}) collective-permute-start(bf16[6,128,128]{2,1,0:T(8,128)(2,1)S(1)} %slice.55), channel_id=1, source_target_pairs={{0,576},{192,0},{384,192},{576,384},{1,577},{193,1},{385,193},{577... | collective-permute-start | bytes 589832 | tf_op jit(solution)/shard_map/ppermute | solution.py:296
  65.5 8.9 %collective-permute-start.5 = (bf16[48,128,128]{2,1,0:T(8,128)(2,1)S(1)}, bf16[48,128,128]{2,1,0:T(8,128)(2,1)S(1)}, u32[]{:S(2)}, u32[]{:S(2)}) collective-permute-start(bf16[48,128,128]{2,1,0:T(8,128)(2,1)S(1)} %constant_dynamic-update-slice_fusion.mine_ref), channel_id=1, source_target_pairs={{0,8},{8,0},{1,9},{9,1},{2,10},{10,2},{3,11},{11,3},{4,12},{12,4},... | collective-permute-start | bytes 4718600 | tf_op jit(solution)/shard_map/ppermute | solution.py:52
  76.1 16.3 %copy-start = (f32[512,128]{1,0:T(8,128)S(1)}, f32[512,128]{1,0:T(8,128)}, u32[]{:S(2)}) copy-start(f32[512,128]{1,0:T(8,128)} %select_add_fusion) | copy-start | bytes 786436
  85.7 25.2 %all-to-all-start.2 = ((bf16[12,128,128]{2,1,0:T(8,128)(2,1)}), bf16[12,128,128]{2,1,0:T(8,128)(2,1)S(1)}, u32[]{:S(2)}, u32[]{:S(2)}) async-start(bf16[12,128,128]{2,1,0:T(8,128)(2,1)} %broadcast_in_dim.13), calls=%async_computation.2 | async-start | bytes 786432 | tf_op jit(solution)/shard_map/all_to_all | solution.py:31
  92.4 8.1 %collective-permute-start.8 = (f32[128,128]{1,0:T(8,128)S(1)}, f32[128,128]{1,0:T(8,128)S(1)}, u32[]{:S(2)}, u32[]{:S(2)}) collective-permute-start(f32[128,128]{1,0:T(8,128)S(1)} %get-tuple-element.42), channel_id=1, source_target_pairs={{0,576},{192,0},{384,192},{576,384},{1,577},{193,1},{385,193},{577... | collective-permute-start | bytes 196616 | tf_op jit(solution)/shard_map/ppermute | solution.py:296
  95.6 6.8 %collective-permute-start.7 = (f32[128,128]{1,0:T(8,128)S(1)}, f32[128,128]{1,0:T(8,128)S(1)}, u32[]{:S(2)}, u32[]{:S(2)}) collective-permute-start(f32[128,128]{1,0:T(8,128)S(1)} %get-tuple-element.43), channel_id=1, source_target_pairs={{0,384},{192,576},{384,0},{576,192},{1,385},{193,577},{385,1},{577... | collective-permute-start | bytes 196616 | tf_op jit(solution)/shard_map/ppermute | solution.py:296
  98.1 6.7 %collective-permute-start.6 = (f32[128,128]{1,0:T(8,128)S(1)}, f32[128,128]{1,0:T(8,128)S(1)}, u32[]{:S(2)}, u32[]{:S(2)}) collective-permute-start(f32[128,128]{1,0:T(8,128)S(1)} %get-tuple-element.41), channel_id=1, source_target_pairs={{0,192},{192,384},{384,576},{576,0},{1,193},{193,385},{385,577},{5... | collective-permute-start | bytes 196616 | tf_op jit(solution)/shard_map/ppermute | solution.py:296
  110.9 11.7 %collective-permute-start.9 = (bf16[12,128,128]{2,1,0:T(8,128)(2,1)S(1)}, bf16[12,128,128]{2,1,0:T(8,128)(2,1)S(1)}, u32[]{:S(2)}, u32[]{:S(2)}) collective-permute-start(bf16[12,128,128]{2,1,0:T(8,128)(2,1)S(1)} %all-to-all-done.2), channel_id=1, source_target_pairs={{0,192},{192,384},{384,576},{576,0},{1,193},{193,385},{385,577},{5... | collective-permute-start | bytes 1179656 | tf_op jit(solution)/shard_map/ppermute | solution.py:296
  112.8 15.8 %collective-permute-start.11 = (bf16[12,128,128]{2,1,0:T(8,128)(2,1)S(1)}, bf16[12,128,128]{2,1,0:T(8,128)(2,1)S(1)}, u32[]{:S(2)}, u32[]{:S(2)}) collective-permute-start(bf16[12,128,128]{2,1,0:T(8,128)(2,1)S(1)} %all-to-all-done.2), channel_id=1, source_target_pairs={{0,576},{192,0},{384,192},{576,384},{1,577},{193,1},{385,193},{577... | collective-permute-start | bytes 1179656 | tf_op jit(solution)/shard_map/ppermute | solution.py:296
  117.4 11.2 %all-to-all-start.3 = ((f32[8,16,128]{2,1,0:T(8,128)}), f32[8,16,128]{2,1,0:T(8,128)S(1)}, u32[]{:S(2)}, u32[]{:S(2)}) async-start(f32[8,16,128]{2,1,0:T(8,128)} %bitcast.16), calls=%async_computation.3 | async-start | bytes 131072 | tf_op jit(solution)/shard_map/all_to_all | solution.py:348
  120.8 85.4 %all-gather.5.cloned.1.call-start = ((), (), s32[]{:S(2)}) async-start(), calls=%async_computation.10 | async-start | bytes 4718592 | tf_op jit(solution)/shard_map/all_gather | solution.py:351
  122.6 8.1 %collective-permute-start.10 = (bf16[6,128,128]{2,1,0:T(8,128)(2,1)S(1)}, bf16[6,128,128]{2,1,0:T(8,128)(2,1)S(1)}, u32[]{:S(2)}, u32[]{:S(2)}) collective-permute-start(bf16[6,128,128]{2,1,0:T(8,128)(2,1)S(1)} %slice.56), channel_id=1, source_target_pairs={{0,192},{192,384},{384,576},{576,0},{1,193},{193,385},{385,577},{5... | collective-permute-start | bytes 589832 | tf_op jit(solution)/shard_map/ppermute | solution.py:296
  128.7 6.8 %collective-permute-start.12 = (bf16[6,128,128]{2,1,0:T(8,128)(2,1)S(1)}, bf16[6,128,128]{2,1,0:T(8,128)(2,1)S(1)}, u32[]{:S(2)}, u32[]{:S(2)}) collective-permute-start(bf16[6,128,128]{2,1,0:T(8,128)(2,1)S(1)} %slice.57), channel_id=1, source_target_pairs={{0,576},{192,0},{384,192},{576,384},{1,577},{193,1},{385,193},{577... | collective-permute-start | bytes 589832 | tf_op jit(solution)/shard_map/ppermute | solution.py:296
  135.6 9.5 %collective-permute-start.13 = (bf16[48,128,128]{2,1,0:T(8,128)(2,1)S(1)}, bf16[48,128,128]{2,1,0:T(8,128)(2,1)S(1)}, u32[]{:S(2)}, u32[]{:S(2)}) collective-permute-start(bf16[48,128,128]{2,1,0:T(8,128)(2,1)S(1)} %constant_dynamic-update-slice_fusion.5.mine_ref), channel_id=1, source_target_pairs={{0,8},{8,0},{1,9},{9,1},{2,10},{10,2},{3,11},{11,3},{4,12},{12,4},... | collective-permute-start | bytes 4718600 | tf_op jit(solution)/shard_map/ppermute | solution.py:52
  147.4 13.8 %all-to-all-start.4 = ((f32[12,16,128]{2,1,0:T(8,128)}), f32[12,16,128]{2,1,0:T(8,128)S(1)}, u32[]{:S(2)}, u32[]{:S(2)}) async-start(f32[12,16,128]{2,1,0:T(8,128)} %broadcast_in_dim.14), calls=%async_computation.4 | async-start | bytes 196608 | tf_op jit(solution)/shard_map/all_to_all | solution.py:31
  156.4 22.7 %copy-start.1 = (f32[512,512]{1,0:T(8,128)S(1)}, f32[512,512]{1,0:T(8,128)}, u32[]{:S(2)}) copy-start(f32[512,512]{1,0:T(8,128)} %param.7) | copy-start | bytes 3145732
  172.3 16.3 %all-to-all-start.6 = ((f32[8,128,128]{2,1,0:T(8,128)}), f32[8,128,128]{2,1,0:T(8,128)S(1)}, u32[]{:S(2)}, u32[]{:S(2)}) async-start(f32[8,128,128]{2,1,0:T(8,128)} %broadcast_in_dim.17), calls=%async_computation.6 | async-start | bytes 1048576 | tf_op jit(solution)/shard_map/all_to_all | solution.py:31
  202.5 15.4 %all-to-all-start.7 = ((f32[8,64,128]{2,1,0:T(8,128)}), f32[8,64,128]{2,1,0:T(8,128)S(1)}, u32[]{:S(2)}, u32[]{:S(2)}) async-start(f32[8,64,128]{2,1,0:T(8,128)} %get-tuple-element.35), calls=%async_computation.7 | async-start | bytes 524288 | tf_op jit(solution)/shard_map/all_to_all | solution.py:369
  217.9 16.4 %all-to-all-start.8 = ((f32[8,64,128]{2,1,0:T(8,128)}), f32[8,64,128]{2,1,0:T(8,128)S(1)}, u32[]{:S(2)}, u32[]{:S(2)}) async-start(f32[8,64,128]{2,1,0:T(8,128)} %solve1.1), calls=%async_computation.8 | async-start | bytes 524288 | tf_op jit(solution)/shard_map/all_to_all | solution.py:369
Sparse Core Ops, SparseCore 0:
  84.2 53.1 all-gather.2
  146.8 53.2 all-gather.4

commit v4 on v3

--- a/solution.py
+++ b/solution.py
@@ -185,10 +185,12 @@
             [jnp.concatenate([value, none], axis=1), jnp.concatenate([none, value], axis=1)], axis=0
         )
 
-    def tile_terms(direction):
+    def tile_terms(direction, step):
         both = pair_rows(direction)
         total = jnp.zeros((rows, 2 * BLK), jnp.float32)
         for c in range(chunks):
+            if low and step == 0:
+                load(2, c).wait()
             table, flip, weights = pieces(c)
             seen = lax.dot_general(both, flip, NN, preferred_element_type=jnp.float32)
             scaled = (seen * weights).astype(jnp.bfloat16)
@@ -218,10 +220,6 @@
             errors = side_ref[:, at]
         total += lax.dot_general(errors, table, NN, preferred_element_type=jnp.float32)
 
-    if low:
-        for c in range(chunks):
-            load(2, c).wait()
-
     grad = local_grad + fold(total)
     resid = -grad
     direction = resid
@@ -229,7 +227,7 @@
     norm_now = jnp.sum(resid * resid, axis=1, keepdims=True)
     for step in range(CG_STEPS):
         local_part = implicit * exact_dot(direction, gram_diag, NN) + ridge_weight * direction
-        image = local_part + tile_terms(direction)
+        image = local_part + tile_terms(direction, step)
         alpha = norm_now / jnp.sum(direction * image, axis=1, keepdims=True)
         delta = delta + alpha * direction
         resid = resid - alpha * image

time: 244 us -> 245 us (level)
  no operation moved by 1% of the time
where the time goes in v4:
time: 245 us; the launch traced here: 243 us
  starting transfers between devices  100 us (41%)
  waiting for transfers between devices  70.9 us (29%)
  Pallas kernels  34.5 us (14%)
  between operations  14.6 us (6%)
  blocking collectives  10.3 us (4%)
  local copies, waits for them, and re-layouts  7.66 us (3%)
  other arithmetic  3.82 us (2%)
    ppermute x11, starting transfers between devices, along_x(): lax.ppermute(value, 'x', [(i, (i + shift) % n_x) for i in range(n_x)])  31.5 us
    pallas_call x2, Pallas kernels, solve(): pl.pallas_call(functools.partial(solve_kernel, block * BLK, implicit, las...  25.7 us
    all_to_all x3, waiting for transfers between devices, spread(): return lax.all_to_all(copies, axis, 0, 0)  19.1 us
    all_to_all x3, starting transfers between devices, spread(): return lax.all_to_all(copies, axis, 0, 0)  17.2 us
    all_to_all x1, starting transfers between devices, spread_first(): return lax.all_to_all(copies, axis, 0, 0)  15.8 us
    ppermute x3, starting transfers between devices, swap_cores(): return lax.ppermute(value, 'core', [(0, 1), (1, 0)])  15.3 us
    ppermute x11, waiting for transfers between devices, along_x(): lax.ppermute(value, 'x', [(i, (i + shift) % n_x) for i in range(n_x)])  13.2 us
    all_to_all x1, waiting for transfers between devices, spread_first(): return lax.all_to_all(copies, axis, 0, 0)  11.7 us
  transfers between devices with their start and end apart: 24, of which 15 were waited for; matrix products, arithmetic and copies ran while one was open for 5% of the time, Pallas kernels for 13%

profile of v4, /device:TPU:1, one launch (start us, length us, event | category | flops | bytes accessed | tf_op | source)
XLA Modules:
  0.0 242.8 jit_solution(4187287933341607498)
XLA Ops:
  6.5 1.8 copies.1
  8.3 15.8 %all-to-all-start = ((bf16[12,128,128]{2,1,0:T(8,128)(2,1)}), bf16[12,128,128]{2,1,0:T(8,128)(2,1)S(1)}, u32[]{:S(2)}, u32[]{:S(2)}) async-start(bf16[12,128,128]{2,1,0:T(8,128)(2,1)} %copies.1), calls=%async_computation | async-start | bytes 786432 | tf_op jit(solution)/shard_map/all_to_all | solution.py:48
  24.2 1.2 fusion
  25.4 2.9 %collective-permute-start = (f32[512,128]{1,0:T(8,128)S(1)}, f32[512,128]{1,0:T(8,128)S(1)}, u32[]{:S(2)}, u32[]{:S(2)}) collective-permute-start(f32[512,128]{1,0:T(8,128)S(1)} %slice_select_fusion), channel_id=1, source_target_pairs={{0,8},{8,0},{1,9},{9,1},{2,10},{10,2},{3,11},{11,3},{4,12},{12,4},... | collective-permute-start | bytes 786440 | tf_op jit(solution)/shard_map/ppermute | solution.py:52
  28.9 0.1 multiply_bitcast_fusion
  29.0 0.1 broadcast_in_dim.12
  29.1 0.1 pad_maximum_fusion
  29.3 1.2 copy.17
  30.4 0.8 select_add_fusion
  31.2 11.7 %all-to-all-done = bf16[12,128,128]{2,1,0:T(8,128)(2,1)S(1)} async-done(((bf16[12,128,128]{2,1,0:T(8,128)(2,1)}), bf16[12,128,128]{2,1,0:T(8,128)(2,1)S(1)}, u32[]{:S(2)}, u32[]{:S(2)}) %all-to-all-start) | async-done | bytes 393248 | tf_op jit(solution)/shard_map/all_to_all | solution.py:48
  42.9 3.1 %collective-permute-start.1 = (bf16[12,128,128]{2,1,0:T(8,128)(2,1)S(1)}, bf16[12,128,128]{2,1,0:T(8,128)(2,1)S(1)}, u32[]{:S(2)}, u32[]{:S(2)}) collective-permute-start(bf16[12,128,128]{2,1,0:T(8,128)(2,1)S(1)} %all-to-all-done), channel_id=1, source_target_pairs={{0,192},{192,384},{384,576},{576,0},{1,193},{193,385},{385,577},{5... | collective-permute-start | bytes 1179656 | tf_op jit(solution)/shard_map/ppermute | solution.py:294
  46.0 3.4 %collective-permute-start.3 = (bf16[12,128,128]{2,1,0:T(8,128)(2,1)S(1)}, bf16[12,128,128]{2,1,0:T(8,128)(2,1)S(1)}, u32[]{:S(2)}, u32[]{:S(2)}) collective-permute-start(bf16[12,128,128]{2,1,0:T(8,128)(2,1)S(1)} %all-to-all-done), channel_id=1, source_target_pairs={{0,576},{192,0},{384,192},{576,384},{1,577},{193,1},{385,193},{577... | collective-permute-start | bytes 1179656 | tf_op jit(solution)/shard_map/ppermute | solution.py:294
  49.4 6.8 %all-to-all-start.1 = ((bf16[8,528,128]{2,1,0:T(8,128)(2,1)}), bf16[8,528,128]{2,1,0:T(8,128)(2,1)}, u32[]{:S(2)}, u32[]{:S(2)}) async-start(bf16[8,528,128]{2,1,0:T(8,128)(2,1)} %bitcast.11), calls=%async_computation.1 | async-start | bytes 2162688 | tf_op jit(solution)/shard_map/all_to_all | solution.py:332
  56.3 1.9 collective-permute-start.2
  58.3 4.6 %collective-permute-start.4 = (bf16[6,128,128]{2,1,0:T(8,128)(2,1)S(1)}, bf16[6,128,128]{2,1,0:T(8,128)(2,1)S(1)}, u32[]{:S(2)}, u32[]{:S(2)}) collective-permute-start(bf16[6,128,128]{2,1,0:T(8,128)(2,1)S(1)} %slice.55), channel_id=1, source_target_pairs={{0,576},{192,0},{384,192},{576,384},{1,577},{193,1},{385,193},{577... | collective-permute-start | bytes 589832 | tf_op jit(solution)/shard_map/ppermute | solution.py:294
  62.9 1.0 collective-permute-done.2
  63.9 1.5 collective-permute-done.4
  65.5 5.9 %collective-permute-start.5 = (bf16[48,128,128]{2,1,0:T(8,128)(2,1)S(1)}, bf16[48,128,128]{2,1,0:T(8,128)(2,1)S(1)}, u32[]{:S(2)}, u32[]{:S(2)}) collective-permute-start(bf16[48,128,128]{2,1,0:T(8,128)(2,1)S(1)} %constant_dynamic-update-slice_fusion.mine_ref), channel_id=1, source_target_pairs={{0,8},{8,0},{1,9},{9,1},{2,10},{10,2},{3,11},{11,3},{4,12},{12,4},... | collective-permute-start | bytes 4718600 | tf_op jit(solution)/shard_map/ppermute | solution.py:52
  71.5 3.0 %collective-permute-done.5.other_ref = bf16[48,128,128]{2,1,0:T(8,128)(2,1)S(1)} collective-permute-done((bf16[48,128,128]{2,1,0:T(8,128)(2,1)S(1)}, bf16[48,128,128]{2,1,0:T(8,128)(2,1)S(1)}, u32[]{:S(2)}, u32[]{:S(2)}) %collective-permute-start.5) | collective-permute-done | bytes 1572896 | tf_op jit(solution)/shard_map/ppermute | solution.py:52
  74.5 1.6 pick.2
  76.1 8.0 %all-to-all-done.1 = bf16[8,528,128]{2,1,0:T(8,128)(2,1)} async-done(((bf16[8,528,128]{2,1,0:T(8,128)(2,1)}), bf16[8,528,128]{2,1,0:T(8,128)(2,1)}, u32[]{:S(2)}, u32[]{:S(2)}) %all-to-all-start.1) | async-done | bytes 1081376 | tf_op jit(solution)/shard_map/all_to_all | solution.py:332
  84.1 0.8 slice.50
  84.9 0.8 broadcast_in_dim.13
  85.7 6.6 %all-to-all-start.2 = ((bf16[12,128,128]{2,1,0:T(8,128)(2,1)}), bf16[12,128,128]{2,1,0:T(8,128)(2,1)S(1)}, u32[]{:S(2)}, u32[]{:S(2)}) async-start(bf16[12,128,128]{2,1,0:T(8,128)(2,1)} %broadcast_in_dim.13), calls=%async_computation.2 | async-start | bytes 786432 | tf_op jit(solution)/shard_map/all_to_all | solution.py:31
  92.4 3.2 %collective-permute-start.8 = (f32[128,128]{1,0:T(8,128)S(1)}, f32[128,128]{1,0:T(8,128)S(1)}, u32[]{:S(2)}, u32[]{:S(2)}) collective-permute-start(f32[128,128]{1,0:T(8,128)S(1)} %get-tuple-element.42), channel_id=1, source_target_pairs={{0,576},{192,0},{384,192},{576,384},{1,577},{193,1},{385,193},{577... | collective-permute-start | bytes 196616 | tf_op jit(solution)/shard_map/ppermute | solution.py:294
  95.6 2.4 %collective-permute-start.7 = (f32[128,128]{1,0:T(8,128)S(1)}, f32[128,128]{1,0:T(8,128)S(1)}, u32[]{:S(2)}, u32[]{:S(2)}) collective-permute-start(f32[128,128]{1,0:T(8,128)S(1)} %get-tuple-element.43), channel_id=1, source_target_pairs={{0,384},{192,576},{384,0},{576,192},{1,385},{193,577},{385,1},{577... | collective-permute-start | bytes 196616 | tf_op jit(solution)/shard_map/ppermute | solution.py:294
  98.1 2.5 %collective-permute-start.6 = (f32[128,128]{1,0:T(8,128)S(1)}, f32[128,128]{1,0:T(8,128)S(1)}, u32[]{:S(2)}, u32[]{:S(2)}) collective-permute-start(f32[128,128]{1,0:T(8,128)S(1)} %get-tuple-element.41), channel_id=1, source_target_pairs={{0,192},{192,384},{384,576},{576,0},{1,193},{193,385},{385,577},{5... | collective-permute-start | bytes 196616 | tf_op jit(solution)/shard_map/ppermute | solution.py:294
  100.6 1.8 collective-permute-done.7
  102.4 2.3 collective-permute-done.6
  104.8 0.6 fusion.3
  105.4 5.5 %all-to-all-done.2 = bf16[12,128,128]{2,1,0:T(8,128)(2,1)S(1)} async-done(((bf16[12,128,128]{2,1,0:T(8,128)(2,1)}), bf16[12,128,128]{2,1,0:T(8,128)(2,1)S(1)}, u32[]{:S(2)}, u32[]{:S(2)}) %all-to-all-start.2) | async-done | bytes 393248 | tf_op jit(solution)/shard_map/all_to_all | solution.py:31
  110.9 1.9 collective-permute-start.9
  112.8 4.6 %collective-permute-start.11 = (bf16[12,128,128]{2,1,0:T(8,128)(2,1)S(1)}, bf16[12,128,128]{2,1,0:T(8,128)(2,1)S(1)}, u32[]{:S(2)}, u32[]{:S(2)}) collective-permute-start(bf16[12,128,128]{2,1,0:T(8,128)(2,1)S(1)} %all-to-all-done.2), channel_id=1, source_target_pairs={{0,576},{192,0},{384,192},{576,384},{1,577},{193,1},{385,193},{577... | collective-permute-start | bytes 1179656 | tf_op jit(solution)/shard_map/ppermute | solution.py:294
  117.4 3.4 %all-to-all-start.3 = ((f32[8,16,128]{2,1,0:T(8,128)}), f32[8,16,128]{2,1,0:T(8,128)S(1)}, u32[]{:S(2)}, u32[]{:S(2)}) async-start(f32[8,16,128]{2,1,0:T(8,128)} %bitcast.16), calls=%async_computation.3 | async-start | bytes 131072 | tf_op jit(solution)/shard_map/all_to_all | solution.py:346
  120.8 1.8 collective-permute-done.9
  122.6 1.9 collective-permute-start.10
  124.6 4.0 %all-to-all-done.3 = f32[8,16,128]{2,1,0:T(8,128)S(1)} async-done(((f32[8,16,128]{2,1,0:T(8,128)}), f32[8,16,128]{2,1,0:T(8,128)S(1)}, u32[]{:S(2)}, u32[]{:S(2)}) %all-to-all-start.3) | async-done | bytes 65568 | tf_op jit(solution)/shard_map/all_to_all | solution.py:346
  128.7 2.0 collective-permute-start.12
  130.6 0.1 constant_dynamic-update-slice_fusion.8
  130.7 4.7 %collective-permute-done.12 = bf16[6,128,128]{2,1,0:T(8,128)(2,1)S(1)} collective-permute-done((bf16[6,128,128]{2,1,0:T(8,128)(2,1)S(1)}, bf16[6,128,128]{2,1,0:T(8,128)(2,1)S(1)}, u32[]{:S(2)}, u32[]{:S(2)}) %collective-permute-start.12) | collective-permute-done | bytes 196640 | tf_op jit(solution)/shard_map/ppermute | solution.py:294
  135.5 0.1 constant_dynamic-update-slice_fusion.5.mine_ref
  135.6 6.5 %collective-permute-start.13 = (bf16[48,128,128]{2,1,0:T(8,128)(2,1)S(1)}, bf16[48,128,128]{2,1,0:T(8,128)(2,1)S(1)}, u32[]{:S(2)}, u32[]{:S(2)}) collective-permute-start(bf16[48,128,128]{2,1,0:T(8,128)(2,1)S(1)} %constant_dynamic-update-slice_fusion.5.mine_ref), channel_id=1, source_target_pairs={{0,8},{8,0},{1,9},{9,1},{2,10},{10,2},{3,11},{11,3},{4,12},{12,4},... | collective-permute-start | bytes 4718600 | tf_op jit(solution)/shard_map/ppermute | solution.py:52
  142.1 3.0 %collective-permute-done.13.other_ref = bf16[48,128,128]{2,1,0:T(8,128)(2,1)S(1)} collective-permute-done((bf16[48,128,128]{2,1,0:T(8,128)(2,1)S(1)}, bf16[48,128,128]{2,1,0:T(8,128)(2,1)S(1)}, u32[]{:S(2)}, u32[]{:S(2)}) %collective-permute-start.13) | collective-permute-done | bytes 1572896 | tf_op jit(solution)/shard_map/ppermute | solution.py:52
  145.1 1.6 pick.3
  146.7 0.6 broadcast_in_dim.14
  147.3 3.7 %all-to-all-start.4 = ((f32[12,16,128]{2,1,0:T(8,128)}), f32[12,16,128]{2,1,0:T(8,128)S(1)}, u32[]{:S(2)}, u32[]{:S(2)}) async-start(f32[12,16,128]{2,1,0:T(8,128)} %broadcast_in_dim.14), calls=%async_computation.4 | async-start | bytes 196608 | tf_op jit(solution)/shard_map/all_to_all | solution.py:31
  151.1 1.0 convert_reduce_fusion
  152.1 0.6 reshape.69.owner_ref
  152.6 3.8 %widen.1.wide_hbm = bf16[128,8192]{1,0:T(8,128)(2,1)} custom-call(s32[128]{0:T(128)} %reshape.69.owner_ref, bf16[8,33,16,128]{3,2,1,0:T(8,128)(2,1)} %bitcast.17.pack_ref.side_hbm), custom_call_target="tpu_custom_call" | custom-call | tf_op jit(solution)/shard_map/widen/pallas_call | solution.py:113
  156.4 4.7 %all-to-all-done.4 = f32[12,16,128]{2,1,0:T(8,128)S(1)} async-done(((f32[12,16,128]{2,1,0:T(8,128)}), f32[12,16,128]{2,1,0:T(8,128)S(1)}, u32[]{:S(2)}, u32[]{:S(2)}) %all-to-all-start.4) | async-done | bytes 98336 | tf_op jit(solution)/shard_map/all_to_all | solution.py:31
  161.2 10.3 %all_to_all.45 = f32[8,16,128]{2,1,0:T(8,128)S(1)} all-to-all(f32[8,16,128]{2,1,0:T(8,128)S(1)} %broadcast_in_dim.15), channel_id=1, replica_groups=mesh['x'=4,'z'=12,'core'=2,'items'=8] {'items'}, dimensions={0} | all-to-all | bytes 131072 | tf_op jit(solution)/shard_map/all_to_all | solution.py:31
  171.5 0.8 broadcast_in_dim.17
  172.3 6.8 %all-to-all-start.6 = ((f32[8,128,128]{2,1,0:T(8,128)}), f32[8,128,128]{2,1,0:T(8,128)S(1)}, u32[]{:S(2)}, u32[]{:S(2)}) async-start(f32[8,128,128]{2,1,0:T(8,128)} %broadcast_in_dim.17), calls=%async_computation.6 | async-start | bytes 1048576 | tf_op jit(solution)/shard_map/all_to_all | solution.py:31
  179.1 0.7 constant_dynamic-slice_fusion
  179.7 8.8 %all-to-all-done.6 = f32[8,128,128]{2,1,0:T(8,128)S(1)} async-done(((f32[8,128,128]{2,1,0:T(8,128)}), f32[8,128,128]{2,1,0:T(8,128)S(1)}, u32[]{:S(2)}, u32[]{:S(2)}) %all-to-all-start.6) | async-done | bytes 524320 | tf_op jit(solution)/shard_map/all_to_all | solution.py:31
  188.6 0.8 fusion.8
  189.4 13.1 %solve0.1 = (f32[8,64,128]{2,1,0:T(8,128)}, f32[64,512]{1,0:T(8,128)}, bf16[128,8192]{1,0:T(8,128)(2,1)}) custom-call(f32[64,512]{1,0:T(8,128)} %bitcast.70, f32[512,128]{1,0:T(8,128)} %bitcast.65, bf16[8192,256]{1,0:T(8,128)(2,1)} %all-gather.3.cloned.1.call-done.table_hbm, bf16[128,8192]{1,0:T(8,128)(2,1)} %widen.1.wide_hbm, ...), custom_call_target="tpu_custom_call" | custom-call | tf_op jit(solution)/shard_map/solve0/pallas_call | solution.py:264
  202.5 3.6 %all-to-all-start.7 = ((f32[8,64,128]{2,1,0:T(8,128)}), f32[8,64,128]{2,1,0:T(8,128)S(1)}, u32[]{:S(2)}, u32[]{:S(2)}) async-start(f32[8,64,128]{2,1,0:T(8,128)} %get-tuple-element.35), calls=%async_computation.7 | async-start | bytes 524288 | tf_op jit(solution)/shard_map/all_to_all | solution.py:367
  206.2 12.6 %solve1.1 = f32[8,64,128]{2,1,0:T(8,128)} custom-call(f32[64,512]{1,0:T(8,128)} %get-tuple-element.36.factors_hbm, f32[512,128]{1,0:T(8,128)} %bitcast.59, bf16[8192,256]{1,0:T(8,128)(2,1)} %all-gather.5.cloned.1.call-done.table_hbm, bf16[128,8192]{1,0:T(8,128)(2,1)} %widen.1.wide_hbm, bf16[128,8192]{1,0:T(8,128)(2,1)} %get-tuple-element.38.side_hbm), custom_call_target="tpu_custom_call" | custom-call | tf_op jit(solution)/shard_map/solve1/pallas_call | solution.py:264
  218.8 6.3 %all-to-all-start.8 = ((f32[8,64,128]{2,1,0:T(8,128)}), f32[8,64,128]{2,1,0:T(8,128)S(1)}, u32[]{:S(2)}, u32[]{:S(2)}) async-start(f32[8,64,128]{2,1,0:T(8,128)} %solve1.1), calls=%async_computation.8 | async-start | bytes 524288 | tf_op jit(solution)/shard_map/all_to_all | solution.py:367
  225.2 0.1 slice.48
  225.3 1.1 pad_maximum_fusion.1
  226.4 8.9 %all-to-all-done.8 = f32[8,64,128]{2,1,0:T(8,128)S(1)} async-done(((f32[8,64,128]{2,1,0:T(8,128)}), f32[8,64,128]{2,1,0:T(8,128)S(1)}, u32[]{:S(2)}, u32[]{:S(2)}) %all-to-all-start.8) | async-done | bytes 262176 | tf_op jit(solution)/shard_map/all_to_all | solution.py:367
  235.3 0.7 constant_dynamic-update-slice_fusion.10
  (47 shorter events, 0.7 us)
Async XLA Ops:
  6.5 22.4 %copy-start.2 = (bf16[1,1,16,128,128]{4,3,2,1,0:T(8,128)(2,1)S(1)}, bf16[1,1,16,128,128]{4,3,2,1,0:T(8,128)(2,1)}, u32[]{:S(2)}) copy-start(bf16[1,1,16,128,128]{4,3,2,1,0:T(8,128)(2,1)} %param.9) | copy-start | bytes 1572868
  8.3 20.7 %copy-start.5 = (s32[1,1,16]{2,1,0:T(1,128)S(1)}, s32[1,1,16]{2,1,0:T(1,128)}, u32[]{:S(2)}) copy-start(s32[1,1,16]{2,1,0:T(1,128)} %param.11) | copy-start | bytes 196
  8.3 20.8 %copy-start.3 = (bf16[1,1,16,128,128]{4,3,2,1,0:T(8,128)(2,1)S(1)}, bf16[1,1,16,128,128]{4,3,2,1,0:T(8,128)(2,1)}, u32[]{:S(2)}) copy-start(bf16[1,1,16,128,128]{4,3,2,1,0:T(8,128)(2,1)} %param.10) | copy-start | bytes 1572868
  8.3 34.5 %all-to-all-start = ((bf16[12,128,128]{2,1,0:T(8,128)(2,1)}), bf16[12,128,128]{2,1,0:T(8,128)(2,1)S(1)}, u32[]{:S(2)}, u32[]{:S(2)}) async-start(bf16[12,128,128]{2,1,0:T(8,128)(2,1)} %copies.1), calls=%async_computation | async-start | bytes 786432 | tf_op jit(solution)/shard_map/all_to_all | solution.py:48
  25.4 5.1 %collective-permute-start = (f32[512,128]{1,0:T(8,128)S(1)}, f32[512,128]{1,0:T(8,128)S(1)}, u32[]{:S(2)}, u32[]{:S(2)}) collective-permute-start(f32[512,128]{1,0:T(8,128)S(1)} %slice_select_fusion), channel_id=1, source_target_pairs={{0,8},{8,0},{1,9},{9,1},{2,10},{10,2},{3,11},{11,3},{4,12},{12,4},... | collective-permute-start | bytes 786440 | tf_op jit(solution)/shard_map/ppermute | solution.py:52
  42.9 13.4 %collective-permute-start.1 = (bf16[12,128,128]{2,1,0:T(8,128)(2,1)S(1)}, bf16[12,128,128]{2,1,0:T(8,128)(2,1)S(1)}, u32[]{:S(2)}, u32[]{:S(2)}) collective-permute-start(bf16[12,128,128]{2,1,0:T(8,128)(2,1)S(1)} %all-to-all-done), channel_id=1, source_target_pairs={{0,192},{192,384},{384,576},{576,0},{1,193},{193,385},{385,577},{5... | collective-permute-start | bytes 1179656 | tf_op jit(solution)/shard_map/ppermute | solution.py:294
  46.0 12.3 %collective-permute-start.3 = (bf16[12,128,128]{2,1,0:T(8,128)(2,1)S(1)}, bf16[12,128,128]{2,1,0:T(8,128)(2,1)S(1)}, u32[]{:S(2)}, u32[]{:S(2)}) collective-permute-start(bf16[12,128,128]{2,1,0:T(8,128)(2,1)S(1)} %all-to-all-done), channel_id=1, source_target_pairs={{0,576},{192,0},{384,192},{576,384},{1,577},{193,1},{385,193},{577... | collective-permute-start | bytes 1179656 | tf_op jit(solution)/shard_map/ppermute | solution.py:294
  49.4 34.7 %all-to-all-start.1 = ((bf16[8,528,128]{2,1,0:T(8,128)(2,1)}), bf16[8,528,128]{2,1,0:T(8,128)(2,1)}, u32[]{:S(2)}, u32[]{:S(2)}) async-start(bf16[8,528,128]{2,1,0:T(8,128)(2,1)} %bitcast.11), calls=%async_computation.1 | async-start | bytes 2162688 | tf_op jit(solution)/shard_map/all_to_all | solution.py:332
  56.2 133.2 %all-gather.3.cloned.1.call-start = ((), (), s32[]{:S(2)}) async-start(), calls=%async_computation.9 | async-start | bytes 4718592 | tf_op jit(solution)/shard_map/all_gather | solution.py:335
  56.3 7.6 %collective-permute-start.2 = (bf16[6,128,128]{2,1,0:T(8,128)(2,1)S(1)}, bf16[6,128,128]{2,1,0:T(8,128)(2,1)S(1)}, u32[]{:S(2)}, u32[]{:S(2)}) collective-permute-start(bf16[6,128,128]{2,1,0:T(8,128)(2,1)S(1)} %slice.54), channel_id=1, source_target_pairs={{0,192},{192,384},{384,576},{576,0},{1,193},{193,385},{385,577},{5... | collective-permute-start | bytes 589832 | tf_op jit(solution)/shard_map/ppermute | solution.py:294
  58.2 13.2 %copy-start.4 = (s32[1,1,16]{2,1,0:T(1,128)S(1)}, s32[1,1,16]{2,1,0:T(1,128)}, u32[]{:S(2)}) copy-start(s32[1,1,16]{2,1,0:T(1,128)} %param.12) | copy-start | bytes 196
  58.3 7.2 %collective-permute-start.4 = (bf16[6,128,128]{2,1,0:T(8,128)(2,1)S(1)}, bf16[6,128,128]{2,1,0:T(8,128)(2,1)S(1)}, u32[]{:S(2)}, u32[]{:S(2)}) collective-permute-start(bf16[6,128,128]{2,1,0:T(8,128)(2,1)S(1)} %slice.55), channel_id=1, source_target_pairs={{0,576},{192,0},{384,192},{576,384},{1,577},{193,1},{385,193},{577... | collective-permute-start | bytes 589832 | tf_op jit(solution)/shard_map/ppermute | solution.py:294
  65.5 8.9 %collective-permute-start.5 = (bf16[48,128,128]{2,1,0:T(8,128)(2,1)S(1)}, bf16[48,128,128]{2,1,0:T(8,128)(2,1)S(1)}, u32[]{:S(2)}, u32[]{:S(2)}) collective-permute-start(bf16[48,128,128]{2,1,0:T(8,128)(2,1)S(1)} %constant_dynamic-update-slice_fusion.mine_ref), channel_id=1, source_target_pairs={{0,8},{8,0},{1,9},{9,1},{2,10},{10,2},{3,11},{11,3},{4,12},{12,4},... | collective-permute-start | bytes 4718600 | tf_op jit(solution)/shard_map/ppermute | solution.py:52
  76.1 16.3 %copy-start = (f32[512,128]{1,0:T(8,128)S(1)}, f32[512,128]{1,0:T(8,128)}, u32[]{:S(2)}) copy-start(f32[512,128]{1,0:T(8,128)} %select_add_fusion) | copy-start | bytes 786436
  85.7 25.2 %all-to-all-start.2 = ((bf16[12,128,128]{2,1,0:T(8,128)(2,1)}), bf16[12,128,128]{2,1,0:T(8,128)(2,1)S(1)}, u32[]{:S(2)}, u32[]{:S(2)}) async-start(bf16[12,128,128]{2,1,0:T(8,128)(2,1)} %broadcast_in_dim.13), calls=%async_computation.2 | async-start | bytes 786432 | tf_op jit(solution)/shard_map/all_to_all | solution.py:31
  92.4 8.1 %collective-permute-start.8 = (f32[128,128]{1,0:T(8,128)S(1)}, f32[128,128]{1,0:T(8,128)S(1)}, u32[]{:S(2)}, u32[]{:S(2)}) collective-permute-start(f32[128,128]{1,0:T(8,128)S(1)} %get-tuple-element.42), channel_id=1, source_target_pairs={{0,576},{192,0},{384,192},{576,384},{1,577},{193,1},{385,193},{577... | collective-permute-start | bytes 196616 | tf_op jit(solution)/shard_map/ppermute | solution.py:294
  95.6 6.8 %collective-permute-start.7 = (f32[128,128]{1,0:T(8,128)S(1)}, f32[128,128]{1,0:T(8,128)S(1)}, u32[]{:S(2)}, u32[]{:S(2)}) collective-permute-start(f32[128,128]{1,0:T(8,128)S(1)} %get-tuple-element.43), channel_id=1, source_target_pairs={{0,384},{192,576},{384,0},{576,192},{1,385},{193,577},{385,1},{577... | collective-permute-start | bytes 196616 | tf_op jit(solution)/shard_map/ppermute | solution.py:294
  98.1 6.7 %collective-permute-start.6 = (f32[128,128]{1,0:T(8,128)S(1)}, f32[128,128]{1,0:T(8,128)S(1)}, u32[]{:S(2)}, u32[]{:S(2)}) collective-permute-start(f32[128,128]{1,0:T(8,128)S(1)} %get-tuple-element.41), channel_id=1, source_target_pairs={{0,192},{192,384},{384,576},{576,0},{1,193},{193,385},{385,577},{5... | collective-permute-start | bytes 196616 | tf_op jit(solution)/shard_map/ppermute | solution.py:294
  110.9 11.7 %collective-permute-start.9 = (bf16[12,128,128]{2,1,0:T(8,128)(2,1)S(1)}, bf16[12,128,128]{2,1,0:T(8,128)(2,1)S(1)}, u32[]{:S(2)}, u32[]{:S(2)}) collective-permute-start(bf16[12,128,128]{2,1,0:T(8,128)(2,1)S(1)} %all-to-all-done.2), channel_id=1, source_target_pairs={{0,192},{192,384},{384,576},{576,0},{1,193},{193,385},{385,577},{5... | collective-permute-start | bytes 1179656 | tf_op jit(solution)/shard_map/ppermute | solution.py:294
  112.8 15.8 %collective-permute-start.11 = (bf16[12,128,128]{2,1,0:T(8,128)(2,1)S(1)}, bf16[12,128,128]{2,1,0:T(8,128)(2,1)S(1)}, u32[]{:S(2)}, u32[]{:S(2)}) collective-permute-start(bf16[12,128,128]{2,1,0:T(8,128)(2,1)S(1)} %all-to-all-done.2), channel_id=1, source_target_pairs={{0,576},{192,0},{384,192},{576,384},{1,577},{193,1},{385,193},{577... | collective-permute-start | bytes 1179656 | tf_op jit(solution)/shard_map/ppermute | solution.py:294
  117.4 11.2 %all-to-all-start.3 = ((f32[8,16,128]{2,1,0:T(8,128)}), f32[8,16,128]{2,1,0:T(8,128)S(1)}, u32[]{:S(2)}, u32[]{:S(2)}) async-start(f32[8,16,128]{2,1,0:T(8,128)} %bitcast.16), calls=%async_computation.3 | async-start | bytes 131072 | tf_op jit(solution)/shard_map/all_to_all | solution.py:346
  120.8 85.4 %all-gather.5.cloned.1.call-start = ((), (), s32[]{:S(2)}) async-start(), calls=%async_computation.10 | async-start | bytes 4718592 | tf_op jit(solution)/shard_map/all_gather | solution.py:349
  122.6 8.1 %collective-permute-start.10 = (bf16[6,128,128]{2,1,0:T(8,128)(2,1)S(1)}, bf16[6,128,128]{2,1,0:T(8,128)(2,1)S(1)}, u32[]{:S(2)}, u32[]{:S(2)}) collective-permute-start(bf16[6,128,128]{2,1,0:T(8,128)(2,1)S(1)} %slice.56), channel_id=1, source_target_pairs={{0,192},{192,384},{384,576},{576,0},{1,193},{193,385},{385,577},{5... | collective-permute-start | bytes 589832 | tf_op jit(solution)/shard_map/ppermute | solution.py:294
  128.7 6.8 %collective-permute-start.12 = (bf16[6,128,128]{2,1,0:T(8,128)(2,1)S(1)}, bf16[6,128,128]{2,1,0:T(8,128)(2,1)S(1)}, u32[]{:S(2)}, u32[]{:S(2)}) collective-permute-start(bf16[6,128,128]{2,1,0:T(8,128)(2,1)S(1)} %slice.57), channel_id=1, source_target_pairs={{0,576},{192,0},{384,192},{576,384},{1,577},{193,1},{385,193},{577... | collective-permute-start | bytes 589832 | tf_op jit(solution)/shard_map/ppermute | solution.py:294
  135.6 9.5 %collective-permute-start.13 = (bf16[48,128,128]{2,1,0:T(8,128)(2,1)S(1)}, bf16[48,128,128]{2,1,0:T(8,128)(2,1)S(1)}, u32[]{:S(2)}, u32[]{:S(2)}) collective-permute-start(bf16[48,128,128]{2,1,0:T(8,128)(2,1)S(1)} %constant_dynamic-update-slice_fusion.5.mine_ref), channel_id=1, source_target_pairs={{0,8},{8,0},{1,9},{9,1},{2,10},{10,2},{3,11},{11,3},{4,12},{12,4},... | collective-permute-start | bytes 4718600 | tf_op jit(solution)/shard_map/ppermute | solution.py:52
  147.3 13.8 %all-to-all-start.4 = ((f32[12,16,128]{2,1,0:T(8,128)}), f32[12,16,128]{2,1,0:T(8,128)S(1)}, u32[]{:S(2)}, u32[]{:S(2)}) async-start(f32[12,16,128]{2,1,0:T(8,128)} %broadcast_in_dim.14), calls=%async_computation.4 | async-start | bytes 196608 | tf_op jit(solution)/shard_map/all_to_all | solution.py:31
  156.4 22.7 %copy-start.1 = (f32[512,512]{1,0:T(8,128)S(1)}, f32[512,512]{1,0:T(8,128)}, u32[]{:S(2)}) copy-start(f32[512,512]{1,0:T(8,128)} %param.7) | copy-start | bytes 3145732
  172.3 16.3 %all-to-all-start.6 = ((f32[8,128,128]{2,1,0:T(8,128)}), f32[8,128,128]{2,1,0:T(8,128)S(1)}, u32[]{:S(2)}, u32[]{:S(2)}) async-start(f32[8,128,128]{2,1,0:T(8,128)} %broadcast_in_dim.17), calls=%async_computation.6 | async-start | bytes 1048576 | tf_op jit(solution)/shard_map/all_to_all | solution.py:31
  202.5 16.3 %all-to-all-start.7 = ((f32[8,64,128]{2,1,0:T(8,128)}), f32[8,64,128]{2,1,0:T(8,128)S(1)}, u32[]{:S(2)}, u32[]{:S(2)}) async-start(f32[8,64,128]{2,1,0:T(8,128)} %get-tuple-element.35), calls=%async_computation.7 | async-start | bytes 524288 | tf_op jit(solution)/shard_map/all_to_all | solution.py:367
  218.8 16.4 %all-to-all-start.8 = ((f32[8,64,128]{2,1,0:T(8,128)}), f32[8,64,128]{2,1,0:T(8,128)S(1)}, u32[]{:S(2)}, u32[]{:S(2)}) async-start(f32[8,64,128]{2,1,0:T(8,128)} %solve1.1), calls=%async_computation.8 | async-start | bytes 524288 | tf_op jit(solution)/shard_map/all_to_all | solution.py:367
Sparse Core Ops, SparseCore 0:
  84.2 53.1 all-gather.2
  146.8 53.2 all-gather.4
